TPU v7x, 128 devices: a whole 4x4x4 slice. The times are simulated.
128 devices in a mesh: row: 8 (over x, core), col: 16 (over y, z).
Axes of the slice: x: 4, y: 4, z: 4, core: 2. Of those that a mesh axis runs over, the one named last changes fastest.
Arguments:
- edge_h: int32 [256, 2048], P('row', 'col'), may hold values from 0 to 7
- edge_v: int32 [256, 2048], P('row', 'col'), may hold values from 0 to 7
- pads: int32 [256, 2048], P('row', 'col'), may hold values 0 or 1
- loads: int32 [256, 256, 2048], P(None, 'row', 'col'), may hold values from 0 to 7
- scales: float32 [256, 8], replicated, may hold values from 0.25 to 4
Outputs:
- drop: float32 [256, 256, 2048], P(None, 'row', 'col')
- res_norms: float32 [256, 5], replicated
All inputs are finite; a program needn't handle non-finite values. No bound on the sum of `pads` on one device may be relied on, other than what follows from the above.
Results may differ from a plain program's by a relative error of at most 0.0003.
Values sent between devices are 32-bit elements; how exact they have to be, the bound alone decides.
No kernel may reach another device: no remote copies, remote signals or barrier semaphores. Data moves between devices by JAX's collectives and lax.ppermute only.
A program may use at most 128 MiB of HBM per device.

v0:
```python
import jax
import jax.numpy as jnp
from jax import lax
from jax.experimental import pallas as pl
from jax.experimental.pallas import tpu as pltpu
from jax.sharding import Mesh
from jax.sharding import PartitionSpec as P

ITERS = 4
ROW = ("x", "core")
COL = ("y", "z")

edge_table = (0.5, 0.8, 1.2, 1.7, 2.3, 3.0, 3.8, 4.7)
load_table = (0.25, 0.5, 1.0, 1.5, 2.0, 3.0, 4.0, 6.0)
pad_conductance = 20.0
leakage = 0.05

LANES = 128
TILE = 8
HALO = ITERS
FIRST = 2 * TILE
LEFT = TILE
COUNT = 2 * ITERS + (ITERS + 1) * (ITERS + 2) // 2
SUMS = 24
MIB = 1024 * 1024
ON_CHIP = pl.BlockSpec(memory_space=pltpu.VMEM)
IN_HBM = pl.BlockSpec(memory_space=pltpu.HBM)


def resident(*shape):
    return pltpu.VMEM(shape, jnp.float32)


def lookup(classes, table):
    total = jnp.zeros(classes.shape, jnp.float32)
    for number, amount in enumerate(table):
        total = total + jnp.where(classes == number, jnp.float32(amount), jnp.float32(0.0))
    return total


def is_even(axes):
    return lax.axis_index(axes[-1]) % 2 == 0


def half_lanes(half):
    return slice(half * LANES, (half + 1) * LANES)


def put(first, second, even, index, low, high):
    first[index] = jnp.where(even, high, low)
    second[index] = jnp.where(even, low, high)


def get(first, second, even, index):
    a, b = first[index], second[index]
    return jnp.where(even, b, a), jnp.where(even, a, b)


def swaps(first, second, axes):
    count = 1
    for axis in axes:
        count *= lax.axis_size(axis)
    later = [(i, i + 1) for i in range(1, count - 1, 2)]
    return (
        lax.ppermute(first, axes, [(i, i ^ 1) for i in range(count)]),
        lax.ppermute(second, axes, later + [(b, a) for a, b in later]),
    )


def prepare_kernel(loads_hbm, scales_ref, eh_ref, ev_ref, pads_ref, rhs_ref, turned_ref, first_ref, second_ref, buf, table_ref, sem):
    scen, rows, cols = loads_hbm.shape
    chunks = rows // TILE

    def copy(chunk):
        source = loads_hbm.at[:, chunk * TILE : (chunk + 1) * TILE, :]
        return pltpu.make_async_copy(source, buf.at[chunk], sem.at[chunk])

    for chunk in range(chunks):
        copy(chunk).start()
    even = is_even(COL)
    classes = jnp.concatenate([eh_ref[...], ev_ref[...], pads_ref[...]], axis=0).astype(jnp.float32)
    classes = jnp.concatenate([classes, jnp.zeros((LANES - 3 * rows, cols), jnp.float32)], axis=0)
    turned_ref[...] = classes.T
    low, high = turned_ref[:TILE, :], turned_ref[cols - TILE :, :]
    put(first_ref, second_ref, even, (rows // 2, slice(None), half_lanes(0)), low, high)
    put(first_ref, second_ref, even, (rows // 2, slice(None), half_lanes(1)), low, high)
    weights = jnp.concatenate(
        [-scales_ref[n : n + 1, :] * jnp.float32(load_table[n]) for n in range(len(load_table))], axis=0
    )
    weights = jnp.concatenate([weights, jnp.zeros((LANES - len(load_table), scen), jnp.float32)], axis=0)
    for half in range(scen // LANES):
        table_ref[half_lanes(half), :] = weights[:, half_lanes(half)].T
    for chunk in range(chunks):
        copy(chunk).wait()
        flat = buf.at[chunk].reshape(scen * TILE, cols)
        for inner in range(TILE):
            row = chunk * TILE + inner
            for half in range(scen // LANES):
                index = flat[pl.ds(half * LANES * TILE + inner, LANES, stride=TILE), :]
                value = jnp.take_along_axis(table_ref[half_lanes(half), :], index, axis=1).T
                rhs_ref[row, :, half_lanes(half)] = value
                at = (row // 2, slice(row % 2 * HALO, (row % 2 + 1) * HALO), half_lanes(half))
                put(first_ref, second_ref, even, at, value[:HALO], value[cols - HALO :])


def prepare(loads, scales, edge_h, edge_v, pads):
    scen, rows, cols = loads.shape
    side = resident(rows // 2 + 1, TILE, scen)
    return pl.pallas_call(
        prepare_kernel,
        in_specs=[IN_HBM] + [ON_CHIP] * 4,
        out_specs=[ON_CHIP] * 4,
        out_shape=[resident(rows, cols, scen), resident(cols, LANES), side, side],
        scratch_shapes=[
            pltpu.VMEM((rows // TILE, scen, TILE, cols), jnp.int32),
            pltpu.VMEM((scen, LANES), jnp.float32),
            pltpu.SemaphoreType.DMA((rows // TILE,)),
        ],
        compiler_params=pltpu.CompilerParams(vmem_limit_bytes=12 * MIB),
        cost_estimate=pl.CostEstimate(flops=20_000_000, bytes_accessed=12 * MIB, transcendentals=0),
    )(loads, scales, edge_h, edge_v, pads)


def message_kernel(rhs_ref, turned_ref, side_a, side_b, first_ref, second_ref):
    rows, cols, scen = rhs_ref.shape
    across = cols // TILE + 1
    even_row, even_col = is_even(ROW), is_even(COL)

    def corner(row, lanes):
        west, east = get(side_a, side_b, even_col, (row // 2, slice(row % 2 * HALO, (row % 2 + 1) * HALO), lanes))
        return jnp.concatenate([east, west], axis=0)

    for row in range(HALO):
        blocks = slice(row * across, row * across + across - 1)
        for half in range(scen // LANES):
            lanes = half_lanes(half)
            low = rhs_ref[row, :, lanes].reshape(across - 1, TILE, LANES)
            high = rhs_ref[rows - HALO + row, :, lanes].reshape(across - 1, TILE, LANES)
            put(first_ref, second_ref, even_row, (blocks, slice(None), lanes), low, high)
            at = (row * across + across - 1, slice(None), lanes)
            put(first_ref, second_ref, even_row, at, corner(row, lanes), corner(rows - HALO + row, lanes))
    west, east = get(side_a, side_b, even_col, (rows // 2, slice(None), half_lanes(0)))
    tiles = [west] + [turned_ref[n * TILE : (n + 1) * TILE, :] for n in range(cols // TILE)] + [east]
    for number, tile in enumerate(tiles):
        at = (HALO * across + number // 2, slice(None), half_lanes(number % 2))
        first_ref[at] = tile
        second_ref[at] = tile


def messages(rhs, turned, side_a, side_b):
    rows, cols, scen = rhs.shape
    tiles = cols // TILE
    out = resident(HALO * (tiles + 1) + (tiles + 2) // 2, TILE, scen)
    return pl.pallas_call(
        message_kernel,
        in_specs=[ON_CHIP] * 4,
        out_specs=[ON_CHIP] * 2,
        out_shape=[out, out],
        compiler_params=pltpu.CompilerParams(vmem_limit_bytes=4 * MIB),
    )(rhs, turned, side_a, side_b)


def conductances(grid, rows, turned_ref, west=None, east=None, north=None, south=None):
    cols = turned_ref.shape[0]
    blank = jnp.zeros((TILE, LANES), jnp.float32)
    side = [blank if piece is None else piece for piece in (west, east)]
    own = jnp.concatenate([blank, side[0], turned_ref[...], side[1], blank], axis=0)
    shape = own.shape
    lane = lax.broadcasted_iota(jnp.int32, shape, 1)

    def classes(array):
        out = pltpu.roll(own, (LEFT - array * rows) % LANES, 1)
        if north is not None:
            above = pltpu.roll(north, (LEFT - (array + 1) * rows) % LANES, 1)
            below = pltpu.roll(south, (LEFT + rows - array * rows) % LANES, 1)
            out = jnp.where(lane < LEFT, above, jnp.where(lane < LEFT + rows, out, below))
        return out

    row_ids = lax.axis_index(ROW) * rows - LEFT + lane
    col_ids = lax.axis_index(COL) * cols - FIRST + lax.broadcasted_iota(jnp.int32, shape, 0)
    all_rows, all_cols = grid
    inside = (row_ids >= 0) & (row_ids < all_rows) & (col_ids >= 0) & (col_ids < all_cols)
    zero = jnp.zeros(shape, jnp.float32)
    g_east = jnp.where(inside & (col_ids < all_cols - 1), lookup(classes(0), edge_table), zero)
    g_south = jnp.where(inside & (row_ids < all_rows - 1), lookup(classes(1), edge_table), zero)
    g_west = pltpu.roll(g_east, 1, 0)
    g_north = pltpu.roll(g_south, 1, 1)
    diagonal = g_east + g_west + g_south + g_north + classes(2) * pad_conductance + leakage
    return g_east, g_south, 1.0 / diagonal, diagonal


def tile_at(tile):
    return pl.ds(pl.multiple_of(tile * TILE, TILE), TILE)


def over(tiles, body):
    if isinstance(tiles, range):
        lax.fori_loop(tiles.start, tiles.stop, lambda tile, carry: (body(tile), carry)[1], 0)
    else:
        for tile in tiles:
            body(tile)


def spread(value, scratch, out, rows, tiles):
    scratch[...] = value

    def body(tile):
        piece = scratch[tile_at(tile), :]
        for row in rows:
            lane = LEFT + row
            out[HALO + row, tile_at(tile), :] = jnp.broadcast_to(piece[:, lane : lane + 1], (TILE, LANES))

    over(tiles, body)


def step(old, new, coef, runs, tiles):
    ge_ref, gs_ref, di_ref, _ = coef
    halves = old.shape[0]

    def body(tile):
        at = tile * TILE
        here, east, west = tile_at(tile), pl.ds(at + 1, TILE), pl.ds(at - 1, TILE)
        for run in runs:
            top = HALO + run[0]
            north = [old[half, top - 1, here, :] for half in range(halves)]
            center = [old[half, top, here, :] for half in range(halves)]
            gn = gs_ref[top - 1, here, :]
            for row in range(top, top + len(run)):
                ge, gw = ge_ref[row, here, :], ge_ref[row, west, :]
                gs, di = gs_ref[row, here, :], di_ref[row, here, :]
                for half in range(halves):
                    south = old[half, row + 1, here, :]
                    total = (ge * old[half, row, east, :] + gw * old[half, row, west, :]) + (
                        gs * south + gn * north[half]
                    )
                    new[half, row, here, :] = total * di
                    north[half], center[half] = center[half], south
                gn = gs

    over(tiles, body)


def gram(fields, coef, half, rows, tiles, sums):
    ge_ref, gs_ref, _, dg_ref = coef
    v = fields[-1]

    def body(tile, sums):
        at = tile * TILE
        here, east, west = tile_at(tile), pl.ds(at + 1, TILE), pl.ds(at - 1, TILE)
        sums = list(sums)
        for own in rows:
            row = HALO + own
            last = (
                ge_ref[row, here, :] * v[half, row, east, :] + ge_ref[row, west, :] * v[half, row, west, :]
            ) + (gs_ref[row, here, :] * v[half, row + 1, here, :] + gs_ref[row - 1, here, :] * v[half, row - 1, here, :])
            dg = dg_ref[row, here, :]
            field = [ref[half, row, here, :] for ref in fields]
            image = [dg * value for value in field] + [last]
            number = 0
            for degree in range(2 * ITERS):
                sums[number] += field[degree // 2] * image[degree - degree // 2]
                number += 1
            for i in range(ITERS + 1):
                for j in range(i, ITERS + 1):
                    sums[number] += image[i] * image[j]
                    number += 1
        return tuple(sums)

    return lax.fori_loop(tiles.start, tiles.stop, body, tuple(sums))


def own_kernel(grid, rhs_ref, turned_ref, ge_ref, gs_ref, di_ref, dg_ref, v0, scratch):
    rows, cols, scen = rhs_ref.shape
    tiles = range(FIRST // TILE, FIRST // TILE + cols // TILE)
    later, below = range(tiles.start + 1, tiles.stop), range(1, rows)
    ge, gs, di, dg = conductances(grid, rows, turned_ref)
    spread(ge, scratch, ge_ref, range(rows), tiles)
    spread(gs, scratch, gs_ref, range(rows), tiles)
    spread(di, scratch, di_ref, below, later)
    spread(dg, scratch, dg_ref, below, later)
    start_own(rhs_ref, di_ref, v0, below, later)


def start_own(rhs_ref, di_ref, v0, rows, tiles):
    def body(tile):
        for row in rows:
            di = di_ref[HALO + row, tile_at(tile), :]
            for half in range(v0.shape[0]):
                value = rhs_ref[row, tile_at(tile - FIRST // TILE), half_lanes(half)]
                v0[half, HALO + row, tile_at(tile), :] = value * di

    over(tiles, body)


def start_side(side_a, side_b, di_ref, v0, rows, cols):
    even = is_even(COL)
    for row in rows:
        for half in range(v0.shape[0]):
            at = (row // 2, slice(row % 2 * HALO, (row % 2 + 1) * HALO), half_lanes(half))
            west, east = get(side_a, side_b, even, at)
            for piece, start in ((west, FIRST - HALO), (east, FIRST + cols)):
                where = slice(start, start + HALO)
                v0[half, HALO + row, where, :] = piece * di_ref[HALO + row, where, :]


def inner_kernel(
    grid, rhs_ref, turned_ref, side_a, side_b, *refs
):
    (ge_ref, gs_ref, di_ref, dg_ref, v0, v1, v2, v3, sums_ref, scratch) = refs[5:]
    coef, fields = (ge_ref, gs_ref, di_ref, dg_ref), (v0, v1, v2, v3)
    rows, cols, scen = rhs_ref.shape
    own = range(FIRST // TILE, FIRST // TILE + cols // TILE)
    low, high = own.start - 1, own.stop
    below = range(1, rows)
    west, east = get(side_a, side_b, is_even(COL), (rows // 2, slice(None), half_lanes(0)))
    ge, gs, di, dg = conductances(grid, rows, turned_ref, west, east)
    spread(ge, scratch, ge_ref, range(rows), (low, high))
    spread(gs, scratch, gs_ref, range(rows), (low, high))
    spread(di, scratch, di_ref, below, (low, own.start, high))
    spread(dg, scratch, dg_ref, below, (own.start,))
    start_own(rhs_ref, di_ref, v0, below, (own.start,))
    start_side(side_a, side_b, di_ref, v0, below, cols)
    for level in range(1, ITERS):
        run = range(1 + level, rows - level)
        step(fields[level - 1], fields[level], coef, (run,), range(low, high + 1))
    for half in range(scen // LANES):
        sums = [jnp.zeros((TILE, LANES), jnp.float32)] * COUNT
        sums = gram(fields, coef, half, range(1 + ITERS, rows - ITERS), own, sums)
        for number, value in enumerate(sums):
            sums_ref[half, number] = value


def outer_kernel(
    grid, rhs_ref, turned_ref, side_a, side_b, end_a, end_b, inner_ref, *refs
):
    (ge_ref, gs_ref, di_ref, dg_ref, v0, v1, v2, v3, sums_ref, scratch) = refs[8:]
    coef, fields = (ge_ref, gs_ref, di_ref, dg_ref), (v0, v1, v2, v3)
    rows, cols, scen = rhs_ref.shape
    own = range(FIRST // TILE, FIRST // TILE + cols // TILE)
    reach = range(own.start - 1, own.stop + 1)
    across = cols // TILE + 1
    even_row = is_even(ROW)
    west, east = get(side_a, side_b, is_even(COL), (rows // 2, slice(None), half_lanes(0)))
    blank = jnp.zeros((TILE, LANES), jnp.float32)
    ends = [[blank], [blank]]
    for number in range(cols // TILE + 2):
        at = (HALO * across + number // 2, slice(None), half_lanes(number % 2))
        for pieces, value in zip(ends, get(end_a, end_b, even_row, at), strict=True):
            pieces.append(value)
    north, south = (jnp.concatenate(pieces + [blank], axis=0) for pieces in ends)
    above, under = range(-HALO, 0), range(rows, rows + HALO)
    ge, gs, di, dg = conductances(grid, rows, turned_ref, west, east, north, south)
    outside = (*above, *under)
    spread(ge, scratch, ge_ref, outside, reach)
    spread(gs, scratch, gs_ref, outside, reach)
    spread(di, scratch, di_ref, (*above, 0, *under), reach)
    spread(dg, scratch, dg_ref, (0,), own)
    start_own(rhs_ref, di_ref, v0, (0,), own)
    start_side(side_a, side_b, di_ref, v0, (0,), cols)
    for number in range(HALO):
        for half in range(scen // LANES):

            def fill(tile, carry, number=number, half=half):
                block = number * across + jnp.where(tile == reach.start, across - 1, tile - own.start)
                pair = get(end_a, end_b, even_row, (block, slice(None), half_lanes(half)))
                for value, row in zip(pair, (HALO + above[number], HALO + under[number]), strict=True):
                    v0[half, row, tile_at(tile), :] = value * di_ref[row, tile_at(tile), :]
                return carry

            lax.fori_loop(reach.start, reach.stop, fill, 0)
    for level in range(1, ITERS):
        runs = (range(level - HALO, level + 1), range(rows - level, rows + HALO - level))
        step(fields[level - 1], fields[level], coef, runs, reach)
    for half in range(scen // LANES):
        sums = [inner_ref[half, number] for number in range(COUNT)]
        sums = gram(fields, coef, half, (*range(ITERS + 1), *range(rows - ITERS, rows)), own, sums)
        for number in range(SUMS):
            value = jnp.sum(sums[number], axis=0, keepdims=True) if number < COUNT else jnp.zeros((1, LANES))
            sums_ref[number : number + 1, half_lanes(half)] = value


def basis(grid, rhs, turned, side):
    rows, cols, scen = rhs.shape
    halves = scen // LANES
    tall, wide = rows + 2 * HALO, cols + 4 * TILE
    coef = [resident(tall, wide, LANES)] * 4
    field = resident(halves, tall, wide, LANES)
    scratch = [pltpu.VMEM((wide, LANES), jnp.float32)]
    params = pltpu.CompilerParams(vmem_limit_bytes=4 * MIB)

    def cost(microseconds):
        return pl.CostEstimate(flops=0, bytes_accessed=int(microseconds * 3.0e6), transcendentals=0)

    *coefs, v0 = pl.pallas_call(
        lambda *refs: own_kernel(grid, *refs),
        in_specs=[ON_CHIP] * 2,
        out_specs=[ON_CHIP] * 5,
        out_shape=coef + [field],
        scratch_shapes=scratch,
        compiler_params=params,
        cost_estimate=cost(8),
    )(rhs, turned)
    partial = resident(halves, SUMS, TILE, LANES)
    *coefs, v0, v1, v2, v3, sums = pl.pallas_call(
        lambda *refs: inner_kernel(grid, *refs),
        in_specs=[ON_CHIP] * 9,
        out_specs=[ON_CHIP] * 9,
        out_shape=coef + [field] * ITERS + [partial],
        scratch_shapes=scratch,
        input_output_aliases={4 + n: n for n in range(5)},
        compiler_params=params,
        cost_estimate=cost(14),
    )(rhs, turned, *side, *coefs, v0)

    def finish(end):
        state = [*coefs, v0, v1, v2, v3]
        *out, total = pl.pallas_call(
            lambda *refs: outer_kernel(grid, *refs),
            in_specs=[ON_CHIP] * 15,
            out_specs=[ON_CHIP] * 9,
            out_shape=coef + [field] * ITERS + [resident(SUMS, scen)],
            scratch_shapes=scratch,
            input_output_aliases={7 + n: n for n in range(8)},
            compiler_params=params,
            cost_estimate=cost(7),
        )(rhs, turned, *side, *end, sums, *state)
        return out[4:], total

    return finish


def coefficients(moment, square):
    count = ITERS + 1

    def product(left, right):
        powers = {}
        for i, a in left.items():
            for j, b in right.items():
                powers[i + j] = powers[i + j] + a * b if i + j in powers else a * b
        total = None
        for power, value in powers.items():
            term = value * moment[power]
            total = term if total is None else total + term
        return total

    def norm(resid):
        total = None
        for i in range(count):
            for j in range(i, count):
                if i in resid and j in resid:
                    term = resid[i] * resid[j] * square[i, j]
                    term = term if i == j else 2.0 * term
                    total = term if total is None else total + term
        return jnp.sqrt(jnp.maximum(total, 0.0))

    def plus(left, factor, right):
        out = dict(left)
        for i, b in right.items():
            out[i] = out[i] + factor * b if i in out else factor * b
        return out

    one = jnp.ones_like(moment[0])
    resid, direction, solution = {0: one}, {0: one}, {}
    gamma = moment[0]
    norms = [jnp.sqrt(square[0, 0])]
    for iteration in range(ITERS):
        image = dict(direction)
        for i, value in direction.items():
            image[i + 1] = image[i + 1] - value if i + 1 in image else -value
        alpha = gamma / product(direction, image)
        solution = plus(solution, alpha, direction)
        resid = plus(resid, -alpha, image)
        norms.append(norm(resid))
        if iteration + 1 < ITERS:
            gamma_new = product(resid, resid)
            direction = plus(resid, gamma_new / gamma, direction)
            gamma = gamma_new
    return [solution[i] for i in range(ITERS)], norms


def combine_kernel(sums_ref, v0, v1, v2, v3, out_hbm, norms_ref, factor_ref, buf, sem):
    scen, rows, cols = out_hbm.shape
    line = lambda n: sums_ref[n : n + 1, :]
    moment = [line(n) for n in range(2 * ITERS)]
    square, number = {}, 2 * ITERS
    for i in range(ITERS + 1):
        for j in range(i, ITERS + 1):
            square[i, j] = line(number)
            number += 1
    factors, norms = coefficients(moment, square)
    for number, value in enumerate(factors):
        factor_ref[number : number + 1, :] = value
    for number, value in enumerate(norms):
        norms_ref[number : number + 1, :] = value

    def copy(chunk):
        target = out_hbm.at[:, chunk * TILE : (chunk + 1) * TILE, :]
        return pltpu.make_async_copy(buf.at[chunk], target, sem.at[chunk])

    for chunk in range(rows // TILE):
        flat = buf.at[chunk].reshape(scen * TILE, cols)
        for inner in range(TILE):
            row = HALO + chunk * TILE + inner
            for half in range(scen // LANES):
                factor = [factor_ref[n : n + 1, half_lanes(half)] for n in range(ITERS)]
                part = [f * v[half, row, FIRST : FIRST + cols, :] for f, v in zip(factor, (v0, v1, v2, v3), strict=True)]
                value = (part[0] + part[1]) + (part[2] + part[3])
                flat[pl.ds(half * LANES * TILE + inner, LANES, stride=TILE), :] = value.T
        copy(chunk).start()
    for chunk in range(rows // TILE):
        copy(chunk).wait()


def combine(sums, fields, scen, rows, cols):
    drop, norms = pl.pallas_call(
        combine_kernel,
        in_specs=[ON_CHIP] * 5,
        out_specs=[IN_HBM, ON_CHIP],
        out_shape=[
            jax.ShapeDtypeStruct((scen, rows, cols), jnp.float32),
            jax.ShapeDtypeStruct((ITERS + 1, scen), jnp.float32),
        ],
        scratch_shapes=[
            pltpu.VMEM((TILE, scen), jnp.float32),
            pltpu.VMEM((rows // TILE, scen, TILE, cols), jnp.float32),
            pltpu.SemaphoreType.DMA((rows // TILE,)),
        ],
        compiler_params=pltpu.CompilerParams(vmem_limit_bytes=8 * MIB),
    )(sums, *fields)
    return drop, norms.T


def sum_everywhere(value):
    for axis in ("core", "z", "y", "x"):
        count = lax.axis_size(axis)
        for flip in (1,) if count == 2 else (1, 3):
            value = value + lax.ppermute(value, axis, [(i, i ^ flip) for i in range(count)])
    return value


def local(edge_h, edge_v, pads, loads, scales):
    scen, rows, cols = loads.shape
    grid = (rows * lax.axis_size(ROW), cols * lax.axis_size(COL))
    rhs, turned, *side = prepare(loads, scales.T, edge_h, edge_v, pads)
    side = swaps(*side, COL)
    finish = basis(grid, rhs, turned, side)
    end = swaps(*messages(rhs, turned, *side), ROW)
    fields, sums = finish(end)
    return combine(sum_everywhere(sums), fields, scen, rows, cols)


def solution(mesh):
    finer = Mesh(mesh.devices.reshape(4, 2, 4, 4), ("x", "core", "y", "z"))
    in_specs = (P(ROW, COL), P(ROW, COL), P(ROW, COL), P(None, ROW, COL), P())
    out_specs = (P(None, ROW, COL), P())
    return jax.shard_map(local, mesh=finer, in_specs=in_specs, out_specs=out_specs, check_vma=False)
```

profile of v0, /device:TPU:0, one launch (start us, length us, event | category | flops | bytes accessed | tf_op | source)
XLA Modules:
  0.0 91.7 jit_solution(344607671542660417)
XLA Ops:
  0.6 0.0 copy-start
  0.6 2.2 %copy-done = s32[256,32,128]{2,1,0:T(8,128)S(1)} copy-done((s32[256,32,128]{2,1,0:T(8,128)S(1)}, s32[256,32,128]{2,1,0:T(8,128)}, u32[]{:S(2)}) %copy-start) | copy-done | bytes 4194328
  2.8 0.0 copy-start.1
  2.8 0.7 copy-done.1
  3.5 0.0 copy-start.2
  3.5 0.7 copy-done.2
  4.3 0.0 copy-start.3
  4.3 0.7 copy-done.3
  5.0 0.0 copy-start.4
  5.0 0.7 copy-done.4
  5.7 4.7 %shard_map.68 = (f32[32,128,256]{2,1,0:T(8,128)S(1)}, f32[128,128]{1,0:T(8,128)S(1)}, f32[17,8,256]{2,1,0:T(8,128)S(1)}, f32[17,8,256]{2,1,0:T(8,128)S(1)}) custom-call(s32[256,32,128]{2,1,0:T(8,128)S(1)} %copy-done, f32[8,256]{1,0:T(8,128)S(1)} %bitcast.2, s32[32,128]{1,0:T(8,128)S(1)} %copy-done.1, s32[32,128]{1,0:T(8,128)S(1)} %copy-done.2, ...), custom_call_target="tpu_custom_call" | custom-call | flops 20000000 | bytes 12582912 | tf_op jit(solution)/shard_map/pallas_call | solution.py:109
  10.4 2.1 %collective-permute-start = (f32[17,8,256]{2,1,0:T(8,128)S(1)}, f32[17,8,256]{2,1,0:T(8,128)S(1)}, u32[]{:S(2)}, u32[]{:S(2)}) collective-permute-start(f32[17,8,256]{2,1,0:T(8,128)S(1)} %get-tuple-element.31), channel_id=1, source_target_pairs={{0,1},{1,0},{2,3},{3,2},{4,5},{5,4},{6,7},{7,6},{8,9},{9,8},{10,11... | collective-permute-start | bytes 417800 | tf_op jit(solution)/shard_map/ppermute | solution.py:65
  12.5 0.7 collective-permute-start.1
  13.2 3.0 %collective-permute-done.side_a.refs_2_ = f32[17,8,256]{2,1,0:T(8,128)S(1)} collective-permute-done((f32[17,8,256]{2,1,0:T(8,128)S(1)}, f32[17,8,256]{2,1,0:T(8,128)S(1)}, u32[]{:S(2)}, u32[]{:S(2)}) %collective-permute-start) | collective-permute-done | bytes 139296 | tf_op jit(solution)/shard_map/ppermute | solution.py:65
  16.2 0.0 collective-permute-done.1.side_b.refs_3_
  16.2 0.1 shard_map.69
  16.3 0.1 collective-permute-start.2
  16.4 0.7 collective-permute-start.3
  17.1 8.4 %shard_map.70 = (f32[40,160,128]{2,1,0:T(8,128)S(1)}, f32[40,160,128]{2,1,0:T(8,128)S(1)}, f32[40,160,128]{2,1,0:T(8,128)S(1)}, f32[40,160,128]{2,1,0:T(8,128)S(1)}, f32[2,40,160,128]{3,2,1,0:T(8,128)S(1)}) custom-call(f32[32,128,256]{2,1,0:T(8,128)S(1)} %get-tuple-element.29.rhs_ref.refs_0_, f32[128,128]{1,0:T(8,128)S(1)} %get-tuple-element.30.turned_ref.refs_1_), custom_call_target="tpu_custom_call" | custom-call | bytes 24000000 | tf_op jit(solution)/shard_map/pallas_call | solution.py:394
  25.4 14.6 %shard_map.71 = (f32[40,160,128]{2,1,0:T(8,128)S(1)}, f32[40,160,128]{2,1,0:T(8,128)S(1)}, f32[40,160,128]{2,1,0:T(8,128)S(1)}, f32[40,160,128]{2,1,0:T(8,128)S(...) custom-call(f32[32,128,256]{2,1,0:T(8,128)S(1)} %get-tuple-element.2, ...), custom_call_target="tpu_custom_call", output_to_operand_aliasing={{0}: (4, {}), {1}: (5, {}), {2}: (6, {}), {3}: (7, {}), {4}... | custom-call | bytes 42000000 | tf_op jit(solution)/shard_map/pallas_call | solution.py:404
  40.1 0.0 collective-permute-done.2.refs_4_
  40.1 0.0 collective-permute-done.3.refs_5_
  40.1 12.8 %shard_map.72 = (f32[40,160,128]{2,1,0:T(8,128)S(1)}, f32[40,160,128]{2,1,0:T(8,128)S(1)}, f32[40,160,128]{2,1,0:T(8,128)S(1)}, f32[40,160,128]{2,1,0:T(8,128)S(...) custom-call(f32[32,128,256]{2,1,0:T(8,128)S(1)} %get-tuple-element.2, ...), custom_call_target="tpu_custom_call", output_to_operand_aliasing={{0}: (7, {}), {1}: (8, {}), {2}: (9, {}), {3}: (10, {}), {4... | custom-call | bytes 21000000 | tf_op jit(solution)/shard_map/pallas_call | solution.py:417
  52.9 2.9 %collective-permute-start.4 = (f32[24,256]{1,0:T(8,128)S(1)}, f32[24,256]{1,0:T(8,128)S(1)}, u32[]{:S(2)}, u32[]{:S(2)}) collective-permute-start(f32[24,256]{1,0:T(8,128)S(1)} %get-tuple-element.49), channel_id=1, source_target_pairs={{0,16},{16,0},{1,17},{17,1},{2,18},{18,2},{3,19},{19,3},{4,20},{20... | collective-permute-start | bytes 73736 | tf_op jit(solution)/shard_map/ppermute | solution.py:537
  55.8 0.8 collective-permute-done.4
  56.7 5.1 %collective-permute-start.5 = (f32[24,256]{1,0:T(8,128)S(1)}, f32[24,256]{1,0:T(8,128)S(1)}, u32[]{:S(2)}, u32[]{:S(2)}) collective-permute-start(f32[24,256]{1,0:T(8,128)S(1)} %add.21), channel_id=1, source_target_pairs={{0,1},{1,0},{2,3},{3,2},{4,5},{5,4},{6,7},{7,6},{8,9},{9,8},{10,11... | collective-permute-start | bytes 73736 | tf_op jit(solution)/shard_map/ppermute | solution.py:537
  61.8 1.8 %collective-permute-done.5 = f32[24,256]{1,0:T(8,128)S(1)} collective-permute-done((f32[24,256]{1,0:T(8,128)S(1)}, f32[24,256]{1,0:T(8,128)S(1)}, u32[]{:S(2)}, u32[]{:S(2)}) %collective-permute-start.5) | collective-permute-done | bytes 24608 | tf_op jit(solution)/shard_map/ppermute | solution.py:537
  63.6 4.8 %collective-permute-start.6 = (f32[24,256]{1,0:T(8,128)S(1)}, f32[24,256]{1,0:T(8,128)S(1)}, u32[]{:S(2)}, u32[]{:S(2)}) collective-permute-start(f32[24,256]{1,0:T(8,128)S(1)} %add.22), channel_id=1, source_target_pairs={{0,3},{1,2},{2,1},{3,0},{4,7},{5,6},{6,5},{7,4},{8,11},{9,10},{10,... | collective-permute-start | bytes 73736 | tf_op jit(solution)/shard_map/ppermute | solution.py:537
  68.5 1.8 %collective-permute-done.6 = f32[24,256]{1,0:T(8,128)S(1)} collective-permute-done((f32[24,256]{1,0:T(8,128)S(1)}, f32[24,256]{1,0:T(8,128)S(1)}, u32[]{:S(2)}, u32[]{:S(2)}) %collective-permute-start.6) | collective-permute-done | bytes 24608 | tf_op jit(solution)/shard_map/ppermute | solution.py:537
  70.3 2.3 %collective-permute-start.7 = (f32[24,256]{1,0:T(8,128)S(1)}, f32[24,256]{1,0:T(8,128)S(1)}, u32[]{:S(2)}, u32[]{:S(2)}) collective-permute-start(f32[24,256]{1,0:T(8,128)S(1)} %add.23), channel_id=1, source_target_pairs={{0,4},{4,0},{8,12},{12,8},{1,5},{5,1},{9,13},{13,9},{2,6},{6,2},{1... | collective-permute-start | bytes 73736 | tf_op jit(solution)/shard_map/ppermute | solution.py:537
  72.6 1.8 %collective-permute-done.7 = f32[24,256]{1,0:T(8,128)S(1)} collective-permute-done((f32[24,256]{1,0:T(8,128)S(1)}, f32[24,256]{1,0:T(8,128)S(1)}, u32[]{:S(2)}, u32[]{:S(2)}) %collective-permute-start.7) | collective-permute-done | bytes 24608 | tf_op jit(solution)/shard_map/ppermute | solution.py:537
  74.4 3.5 %collective-permute-start.8 = (f32[24,256]{1,0:T(8,128)S(1)}, f32[24,256]{1,0:T(8,128)S(1)}, u32[]{:S(2)}, u32[]{:S(2)}) collective-permute-start(f32[24,256]{1,0:T(8,128)S(1)} %add.24), channel_id=1, source_target_pairs={{0,12},{4,8},{8,4},{12,0},{1,13},{5,9},{9,5},{13,1},{2,14},{6,10},... | collective-permute-start | bytes 73736 | tf_op jit(solution)/shard_map/ppermute | solution.py:537
  77.8 1.8 %collective-permute-done.8 = f32[24,256]{1,0:T(8,128)S(1)} collective-permute-done((f32[24,256]{1,0:T(8,128)S(1)}, f32[24,256]{1,0:T(8,128)S(1)}, u32[]{:S(2)}, u32[]{:S(2)}) %collective-permute-start.8) | collective-permute-done | bytes 24608 | tf_op jit(solution)/shard_map/ppermute | solution.py:537
  79.6 1.5 %collective-permute-start.9 = (f32[24,256]{1,0:T(8,128)S(1)}, f32[24,256]{1,0:T(8,128)S(1)}, u32[]{:S(2)}, u32[]{:S(2)}) collective-permute-start(f32[24,256]{1,0:T(8,128)S(1)} %add.25), channel_id=1, source_target_pairs={{0,32},{32,0},{64,96},{96,64},{1,33},{33,1},{65,97},{97,65},{2,34}... | collective-permute-start | bytes 73736 | tf_op jit(solution)/shard_map/ppermute | solution.py:537
  81.1 2.3 %collective-permute-done.9 = f32[24,256]{1,0:T(8,128)S(1)} collective-permute-done((f32[24,256]{1,0:T(8,128)S(1)}, f32[24,256]{1,0:T(8,128)S(1)}, u32[]{:S(2)}, u32[]{:S(2)}) %collective-permute-start.9) | collective-permute-done | bytes 24608 | tf_op jit(solution)/shard_map/ppermute | solution.py:537
  83.5 2.4 %collective-permute-start.10 = (f32[24,256]{1,0:T(8,128)S(1)}, f32[24,256]{1,0:T(8,128)S(1)}, u32[]{:S(2)}, u32[]{:S(2)}) collective-permute-start(f32[24,256]{1,0:T(8,128)S(1)} %add.26), channel_id=1, source_target_pairs={{0,96},{32,64},{64,32},{96,0},{1,97},{33,65},{65,33},{97,1},{2,98}... | collective-permute-start | bytes 73736 | tf_op jit(solution)/shard_map/ppermute | solution.py:537
  85.9 2.6 %collective-permute-done.10 = f32[24,256]{1,0:T(8,128)S(1)} collective-permute-done((f32[24,256]{1,0:T(8,128)S(1)}, f32[24,256]{1,0:T(8,128)S(1)}, u32[]{:S(2)}, u32[]{:S(2)}) %collective-permute-start.10) | collective-permute-done | bytes 24608 | tf_op jit(solution)/shard_map/ppermute | solution.py:537
  88.5 3.2 %shard_map.73 = (f32[256,32,128]{2,1,0:T(8,128)}, f32[5,256]{1,0:T(8,128)}) custom-call(f32[24,256]{1,0:T(8,128)S(1)} %add.27.sums_ref, f32[2,40,160,128]{3,2,1,0:T(8,128)S(1)} %get-tuple-element.50.v0, f32[2,40,160,128]{3,2,1,0:T(8,128)S(1)} %get-tuple-element.51.v1, f32[2,40,160,128]{3,2,1,0:T(8,128)S(1)} %get-tuple-element.52.v2, ...), custom_call_target="tpu_custom_call" | custom-call | tf_op jit(solution)/shard_map/pallas_call | solution.py:515
  (7 shorter events, 0.0 us)
Async XLA Ops:
  0.6 2.2 %copy-start = (s32[256,32,128]{2,1,0:T(8,128)S(1)}, s32[256,32,128]{2,1,0:T(8,128)}, u32[]{:S(2)}) copy-start(s32[256,32,128]{2,1,0:T(8,128)} %loads_hbm.1) | copy-start | bytes 12582916
  2.8 0.7 copy-start.1
  3.5 0.7 copy-start.2
  4.3 0.7 copy-start.3
  5.0 0.7 copy-start.4
  10.4 5.8 %collective-permute-start = (f32[17,8,256]{2,1,0:T(8,128)S(1)}, f32[17,8,256]{2,1,0:T(8,128)S(1)}, u32[]{:S(2)}, u32[]{:S(2)}) collective-permute-start(f32[17,8,256]{2,1,0:T(8,128)S(1)} %get-tuple-element.31), channel_id=1, source_target_pairs={{0,1},{1,0},{2,3},{3,2},{4,5},{5,4},{6,7},{7,6},{8,9},{9,8},{10,11... | collective-permute-start | bytes 417800 | tf_op jit(solution)/shard_map/ppermute | solution.py:65
  12.5 3.7 %collective-permute-start.1 = (f32[17,8,256]{2,1,0:T(8,128)S(1)}, f32[17,8,256]{2,1,0:T(8,128)S(1)}, u32[]{:S(2)}, u32[]{:S(2)}) collective-permute-start(f32[17,8,256]{2,1,0:T(8,128)S(1)} %get-tuple-element.32), channel_id=1, source_target_pairs={{1,2},{3,4},{5,6},{7,8},{9,10},{11,12},{13,14},{2,1},{4,3},{6,5},{... | collective-permute-start | bytes 417800 | tf_op jit(solution)/shard_map/ppermute | solution.py:66
  16.3 23.8 %collective-permute-start.2 = (f32[77,8,256]{2,1,0:T(8,128)S(1)}, f32[77,8,256]{2,1,0:T(8,128)S(1)}, u32[]{:S(2)}, u32[]{:S(2)}) collective-permute-start(f32[77,8,256]{2,1,0:T(8,128)S(1)} %get-tuple-element.33), channel_id=1, source_target_pairs={{0,16},{16,0},{32,48},{48,32},{64,80},{80,64},{96,112},{112,96},{1... | collective-permute-start | bytes 1892360 | tf_op jit(solution)/shard_map/ppermute | solution.py:65
  16.4 23.7 %collective-permute-start.3 = (f32[77,8,256]{2,1,0:T(8,128)S(1)}, f32[77,8,256]{2,1,0:T(8,128)S(1)}, u32[]{:S(2)}, u32[]{:S(2)}) collective-permute-start(f32[77,8,256]{2,1,0:T(8,128)S(1)} %get-tuple-element.34), channel_id=1, source_target_pairs={{16,32},{48,64},{80,96},{32,16},{64,48},{96,80},{17,33},{49,65},{8... | collective-permute-start | bytes 1892360 | tf_op jit(solution)/shard_map/ppermute | solution.py:66
  52.9 3.7 %collective-permute-start.4 = (f32[24,256]{1,0:T(8,128)S(1)}, f32[24,256]{1,0:T(8,128)S(1)}, u32[]{:S(2)}, u32[]{:S(2)}) collective-permute-start(f32[24,256]{1,0:T(8,128)S(1)} %get-tuple-element.49), channel_id=1, source_target_pairs={{0,16},{16,0},{1,17},{17,1},{2,18},{18,2},{3,19},{19,3},{4,20},{20... | collective-permute-start | bytes 73736 | tf_op jit(solution)/shard_map/ppermute | solution.py:537
  56.7 6.9 %collective-permute-start.5 = (f32[24,256]{1,0:T(8,128)S(1)}, f32[24,256]{1,0:T(8,128)S(1)}, u32[]{:S(2)}, u32[]{:S(2)}) collective-permute-start(f32[24,256]{1,0:T(8,128)S(1)} %add.21), channel_id=1, source_target_pairs={{0,1},{1,0},{2,3},{3,2},{4,5},{5,4},{6,7},{7,6},{8,9},{9,8},{10,11... | collective-permute-start | bytes 73736 | tf_op jit(solution)/shard_map/ppermute | solution.py:537
  63.6 6.7 %collective-permute-start.6 = (f32[24,256]{1,0:T(8,128)S(1)}, f32[24,256]{1,0:T(8,128)S(1)}, u32[]{:S(2)}, u32[]{:S(2)}) collective-permute-start(f32[24,256]{1,0:T(8,128)S(1)} %add.22), channel_id=1, source_target_pairs={{0,3},{1,2},{2,1},{3,0},{4,7},{5,6},{6,5},{7,4},{8,11},{9,10},{10,... | collective-permute-start | bytes 73736 | tf_op jit(solution)/shard_map/ppermute | solution.py:537
  70.3 4.1 %collective-permute-start.7 = (f32[24,256]{1,0:T(8,128)S(1)}, f32[24,256]{1,0:T(8,128)S(1)}, u32[]{:S(2)}, u32[]{:S(2)}) collective-permute-start(f32[24,256]{1,0:T(8,128)S(1)} %add.23), channel_id=1, source_target_pairs={{0,4},{4,0},{8,12},{12,8},{1,5},{5,1},{9,13},{13,9},{2,6},{6,2},{1... | collective-permute-start | bytes 73736 | tf_op jit(solution)/shard_map/ppermute | solution.py:537
  74.4 5.3 %collective-permute-start.8 = (f32[24,256]{1,0:T(8,128)S(1)}, f32[24,256]{1,0:T(8,128)S(1)}, u32[]{:S(2)}, u32[]{:S(2)}) collective-permute-start(f32[24,256]{1,0:T(8,128)S(1)} %add.24), channel_id=1, source_target_pairs={{0,12},{4,8},{8,4},{12,0},{1,13},{5,9},{9,5},{13,1},{2,14},{6,10},... | collective-permute-start | bytes 73736 | tf_op jit(solution)/shard_map/ppermute | solution.py:537
  79.6 3.8 %collective-permute-start.9 = (f32[24,256]{1,0:T(8,128)S(1)}, f32[24,256]{1,0:T(8,128)S(1)}, u32[]{:S(2)}, u32[]{:S(2)}) collective-permute-start(f32[24,256]{1,0:T(8,128)S(1)} %add.25), channel_id=1, source_target_pairs={{0,32},{32,0},{64,96},{96,64},{1,33},{33,1},{65,97},{97,65},{2,34}... | collective-permute-start | bytes 73736 | tf_op jit(solution)/shard_map/ppermute | solution.py:537
  83.5 5.0 %collective-permute-start.10 = (f32[24,256]{1,0:T(8,128)S(1)}, f32[24,256]{1,0:T(8,128)S(1)}, u32[]{:S(2)}, u32[]{:S(2)}) collective-permute-start(f32[24,256]{1,0:T(8,128)S(1)} %add.26), channel_id=1, source_target_pairs={{0,96},{32,64},{64,32},{96,0},{1,97},{33,65},{65,33},{97,1},{2,98}... | collective-permute-start | bytes 73736 | tf_op jit(solution)/shard_map/ppermute | solution.py:537
where the time goes:
time: 92.3 us; the launch traced here: 91.7 us
  Pallas kernels  43.8 us (47%)
  starting transfers between devices  26.1 us (28%)
  waiting for transfers between devices  16 us (17%)
  local copies, waits for them, and re-layouts  5.03 us (5%)
    ppermute x7, starting transfers between devices, sum_everywhere(): lax.ppermute(value, axis, [(i, i ^ flip) for i in range(count)])  22.5 us
    pallas_call x1, Pallas kernels, basis(): pl.pallas_call(lambda *refs: inner_kernel(grid, *refs), in_specs=[ON_CHIP...  14.6 us
    ppermute x7, waiting for transfers between devices, sum_everywhere(): lax.ppermute(value, axis, [(i, i ^ flip) for i in range(count)])  13 us
    pallas_call x1, Pallas kernels, finish(): pl.pallas_call(lambda *refs: outer_kernel(grid, *refs), in_specs=[ON_CHIP...  12.8 us
    pallas_call x1, Pallas kernels, basis(): pl.pallas_call(lambda *refs: own_kernel(grid, *refs), in_specs=[ON_CHIP]...  8.36 us
    unnamed x10, local copies, waits for them, and re-layouts  5.03 us
    pallas_call x1, Pallas kernels, prepare(): pl.pallas_call(prepare_kernel, in_specs=[IN_HBM] + [ON_CHIP] * 4, out_spe...  4.73 us
    pallas_call x1, Pallas kernels, combine(): pl.pallas_call(combine_kernel, in_specs=[ON_CHIP] * 5, out_specs=[IN_HBM,...  3.2 us
  transfers between devices with their start and end apart: 11, of which 8 were waited for; matrix products, arithmetic and copies ran while one was open for 0% of the time, Pallas kernels for 25%

commit v1 on v0

--- a/solution.py
+++ b/solution.py
@@ -67,9 +67,27 @@
     )
 
 
-def prepare_kernel(loads_hbm, scales_ref, eh_ref, ev_ref, pads_ref, rhs_ref, turned_ref, first_ref, second_ref, buf, table_ref, sem):
+def pick(table, classes):
+    bit = 1
+    while len(table) > 1:
+        odd = (classes & bit) != 0
+        table = [jnp.where(odd, table[n + 1], table[n]) for n in range(0, len(table), 2)]
+        bit *= 2
+    return table[0]
+
+
+def prepare_kernel(
+    loads_hbm, scales_hbm, eh_hbm, ev_hbm, pads_hbm, rhs_ref, turned_ref, first_ref, second_ref,
+    buf, scales_ref, classes_ref, sem, small_sem,
+):
     scen, rows, cols = loads_hbm.shape
     chunks = rows // TILE
+    small = [pltpu.make_async_copy(scales_hbm, scales_ref, small_sem.at[3])]
+    for array, source in enumerate((eh_hbm, ev_hbm, pads_hbm)):
+        target = classes_ref.at[array * rows : (array + 1) * rows, :]
+        small.append(pltpu.make_async_copy(source, target, small_sem.at[array]))
+    for one in small:
+        one.start()
 
     def copy(chunk):
         source = loads_hbm.at[:, chunk * TILE : (chunk + 1) * TILE, :]
@@ -78,7 +96,9 @@
     for chunk in range(chunks):
         copy(chunk).start()
     even = is_even(COL)
-    classes = jnp.concatenate([eh_ref[...], ev_ref[...], pads_ref[...]], axis=0).astype(jnp.float32)
+    for one in small:
+        one.wait()
+    classes = classes_ref[...].astype(jnp.float32)
     classes = jnp.concatenate([classes, jnp.zeros((LANES - 3 * rows, cols), jnp.float32)], axis=0)
     turned_ref[...] = classes.T
     low, high = turned_ref[:TILE, :], turned_ref[cols - TILE :, :]
@@ -87,9 +107,6 @@
     weights = jnp.concatenate(
         [-scales_ref[n : n + 1, :] * jnp.float32(load_table[n]) for n in range(len(load_table))], axis=0
     )
-    weights = jnp.concatenate([weights, jnp.zeros((LANES - len(load_table), scen), jnp.float32)], axis=0)
-    for half in range(scen // LANES):
-        table_ref[half_lanes(half), :] = weights[:, half_lanes(half)].T
     for chunk in range(chunks):
         copy(chunk).wait()
         flat = buf.at[chunk].reshape(scen * TILE, cols)
@@ -97,7 +114,7 @@
             row = chunk * TILE + inner
             for half in range(scen // LANES):
                 index = flat[pl.ds(half * LANES * TILE + inner, LANES, stride=TILE), :]
-                value = jnp.take_along_axis(table_ref[half_lanes(half), :], index, axis=1).T
+                value = pick([weights[n : n + 1, half_lanes(half)] for n in range(8)], index.T)
                 rhs_ref[row, :, half_lanes(half)] = value
                 at = (row // 2, slice(row % 2 * HALO, (row % 2 + 1) * HALO), half_lanes(half))
                 put(first_ref, second_ref, even, at, value[:HALO], value[cols - HALO :])
@@ -108,20 +125,22 @@
     side = resident(rows // 2 + 1, TILE, scen)
     return pl.pallas_call(
         prepare_kernel,
-        in_specs=[IN_HBM] + [ON_CHIP] * 4,
+        in_specs=[IN_HBM] * 5,
         out_specs=[ON_CHIP] * 4,
         out_shape=[resident(rows, cols, scen), resident(cols, LANES), side, side],
         scratch_shapes=[
             pltpu.VMEM((rows // TILE, scen, TILE, cols), jnp.int32),
-            pltpu.VMEM((scen, LANES), jnp.float32),
+            pltpu.VMEM(scales.shape, jnp.float32),
+            pltpu.VMEM((3 * rows, cols), jnp.int32),
             pltpu.SemaphoreType.DMA((rows // TILE,)),
+            pltpu.SemaphoreType.DMA((4,)),
         ],
         compiler_params=pltpu.CompilerParams(vmem_limit_bytes=12 * MIB),
         cost_estimate=pl.CostEstimate(flops=20_000_000, bytes_accessed=12 * MIB, transcendentals=0),
-    )(loads, scales, edge_h, edge_v, pads)
-
-
-def message_kernel(rhs_ref, turned_ref, side_a, side_b, first_ref, second_ref):
+    )(*(pltpu.with_memory_space_constraint(a, pltpu.HBM) for a in (loads, scales, edge_h, edge_v, pads)))
+
+
+def message_kernel(rhs_ref, turned_ref, side_a, side_b, _, first_ref, second_ref):
     rows, cols, scen = rhs_ref.shape
     across = cols // TILE + 1
     even_row, even_col = is_even(ROW), is_even(COL)
@@ -147,17 +166,17 @@
         second_ref[at] = tile
 
 
-def messages(rhs, turned, side_a, side_b):
+def messages(rhs, turned, side_a, side_b, after):
     rows, cols, scen = rhs.shape
     tiles = cols // TILE
     out = resident(HALO * (tiles + 1) + (tiles + 2) // 2, TILE, scen)
     return pl.pallas_call(
         message_kernel,
-        in_specs=[ON_CHIP] * 4,
+        in_specs=[ON_CHIP] * 5,
         out_specs=[ON_CHIP] * 2,
         out_shape=[out, out],
         compiler_params=pltpu.CompilerParams(vmem_limit_bytes=4 * MIB),
-    )(rhs, turned, side_a, side_b)
+    )(rhs, turned, side_a, side_b, after)
 
 
 def conductances(grid, rows, turned_ref, west=None, east=None, north=None, south=None):
@@ -190,30 +209,34 @@
 
 
 def tile_at(tile):
+    if isinstance(tile, int):
+        return slice(tile * TILE, (tile + 1) * TILE)
     return pl.ds(pl.multiple_of(tile * TILE, TILE), TILE)
 
 
-def over(tiles, body):
-    if isinstance(tiles, range):
-        lax.fori_loop(tiles.start, tiles.stop, lambda tile, carry: (body(tile), carry)[1], 0)
-    else:
+def over(tiles, body, together=1):
+    if len(tiles) <= together:
         for tile in tiles:
             body(tile)
-
-
-def spread(value, scratch, out, rows, tiles):
-    scratch[...] = value
-
-    def body(tile):
-        piece = scratch[tile_at(tile), :]
+        return
+
+    def turn(number, carry):
+        for extra in range(together):
+            body(tiles.start + number * together + extra)
+        return carry
+
+    lax.fori_loop(0, len(tiles) // together, turn, 0)
+
+
+def spread(value, out, rows, tiles):
+    for tile in tiles:
+        piece = value[tile * TILE : (tile + 1) * TILE, :]
         for row in rows:
             lane = LEFT + row
             out[HALO + row, tile_at(tile), :] = jnp.broadcast_to(piece[:, lane : lane + 1], (TILE, LANES))
 
-    over(tiles, body)
-
-
-def step(old, new, coef, runs, tiles):
+
+def step(old, new, coef, runs, tiles, together=1):
     ge_ref, gs_ref, di_ref, _ = coef
     halves = old.shape[0]
 
@@ -237,7 +260,7 @@
                     north[half], center[half] = center[half], south
                 gn = gs
 
-    over(tiles, body)
+    over(tiles, body, together)
 
 
 def gram(fields, coef, half, rows, tiles, sums):
@@ -269,19 +292,19 @@
     return lax.fori_loop(tiles.start, tiles.stop, body, tuple(sums))
 
 
-def own_kernel(grid, rhs_ref, turned_ref, ge_ref, gs_ref, di_ref, dg_ref, v0, scratch):
+def own_kernel(grid, rhs_ref, turned_ref, ge_ref, gs_ref, di_ref, dg_ref, v0):
     rows, cols, scen = rhs_ref.shape
     tiles = range(FIRST // TILE, FIRST // TILE + cols // TILE)
     later, below = range(tiles.start + 1, tiles.stop), range(1, rows)
     ge, gs, di, dg = conductances(grid, rows, turned_ref)
-    spread(ge, scratch, ge_ref, range(rows), tiles)
-    spread(gs, scratch, gs_ref, range(rows), tiles)
-    spread(di, scratch, di_ref, below, later)
-    spread(dg, scratch, dg_ref, below, later)
+    spread(ge, ge_ref, range(rows), tiles)
+    spread(gs, gs_ref, range(rows), tiles)
+    spread(di, di_ref, below, later)
+    spread(dg, dg_ref, below, later)
     start_own(rhs_ref, di_ref, v0, below, later)
 
 
-def start_own(rhs_ref, di_ref, v0, rows, tiles):
+def start_own(rhs_ref, di_ref, v0, rows, tiles, together=1):
     def body(tile):
         for row in rows:
             di = di_ref[HALO + row, tile_at(tile), :]
@@ -289,7 +312,7 @@
                 value = rhs_ref[row, tile_at(tile - FIRST // TILE), half_lanes(half)]
                 v0[half, HALO + row, tile_at(tile), :] = value * di
 
-    over(tiles, body)
+    over(tiles, body, together)
 
 
 def start_side(side_a, side_b, di_ref, v0, rows, cols):
@@ -306,7 +329,7 @@
 def inner_kernel(
     grid, rhs_ref, turned_ref, side_a, side_b, *refs
 ):
-    (ge_ref, gs_ref, di_ref, dg_ref, v0, v1, v2, v3, sums_ref, scratch) = refs[5:]
+    (ge_ref, gs_ref, di_ref, dg_ref, v0, v1, v2, v3, sums_ref) = refs[5:]
     coef, fields = (ge_ref, gs_ref, di_ref, dg_ref), (v0, v1, v2, v3)
     rows, cols, scen = rhs_ref.shape
     own = range(FIRST // TILE, FIRST // TILE + cols // TILE)
@@ -314,11 +337,11 @@
     below = range(1, rows)
     west, east = get(side_a, side_b, is_even(COL), (rows // 2, slice(None), half_lanes(0)))
     ge, gs, di, dg = conductances(grid, rows, turned_ref, west, east)
-    spread(ge, scratch, ge_ref, range(rows), (low, high))
-    spread(gs, scratch, gs_ref, range(rows), (low, high))
-    spread(di, scratch, di_ref, below, (low, own.start, high))
-    spread(dg, scratch, dg_ref, below, (own.start,))
-    start_own(rhs_ref, di_ref, v0, below, (own.start,))
+    spread(ge, ge_ref, range(rows), (low, high))
+    spread(gs, gs_ref, range(rows), (low, high))
+    spread(di, di_ref, below, (low, own.start, high))
+    spread(dg, dg_ref, below, (own.start,))
+    start_own(rhs_ref, di_ref, v0, below, range(own.start, own.start + 1))
     start_side(side_a, side_b, di_ref, v0, below, cols)
     for level in range(1, ITERS):
         run = range(1 + level, rows - level)
@@ -333,7 +356,7 @@
 def outer_kernel(
     grid, rhs_ref, turned_ref, side_a, side_b, end_a, end_b, inner_ref, *refs
 ):
-    (ge_ref, gs_ref, di_ref, dg_ref, v0, v1, v2, v3, sums_ref, scratch) = refs[8:]
+    (ge_ref, gs_ref, di_ref, dg_ref, v0, v1, v2, v3, sums_ref) = refs[8:]
     coef, fields = (ge_ref, gs_ref, di_ref, dg_ref), (v0, v1, v2, v3)
     rows, cols, scen = rhs_ref.shape
     own = range(FIRST // TILE, FIRST // TILE + cols // TILE)
@@ -351,26 +374,22 @@
     above, under = range(-HALO, 0), range(rows, rows + HALO)
     ge, gs, di, dg = conductances(grid, rows, turned_ref, west, east, north, south)
     outside = (*above, *under)
-    spread(ge, scratch, ge_ref, outside, reach)
-    spread(gs, scratch, gs_ref, outside, reach)
-    spread(di, scratch, di_ref, (*above, 0, *under), reach)
-    spread(dg, scratch, dg_ref, (0,), own)
-    start_own(rhs_ref, di_ref, v0, (0,), own)
+    spread(ge, ge_ref, outside, reach)
+    spread(gs, gs_ref, outside, reach)
+    spread(di, di_ref, (*above, 0, *under), reach)
+    spread(dg, dg_ref, (0,), own)
+    start_own(rhs_ref, di_ref, v0, (0,), own, len(own))
     start_side(side_a, side_b, di_ref, v0, (0,), cols)
     for number in range(HALO):
         for half in range(scen // LANES):
-
-            def fill(tile, carry, number=number, half=half):
-                block = number * across + jnp.where(tile == reach.start, across - 1, tile - own.start)
+            for tile in reach:
+                block = number * across + (across - 1 if tile == reach.start else tile - own.start)
                 pair = get(end_a, end_b, even_row, (block, slice(None), half_lanes(half)))
                 for value, row in zip(pair, (HALO + above[number], HALO + under[number]), strict=True):
                     v0[half, row, tile_at(tile), :] = value * di_ref[row, tile_at(tile), :]
-                return carry
-
-            lax.fori_loop(reach.start, reach.stop, fill, 0)
     for level in range(1, ITERS):
         runs = (range(level - HALO, level + 1), range(rows - level, rows + HALO - level))
-        step(fields[level - 1], fields[level], coef, runs, reach)
+        step(fields[level - 1], fields[level], coef, runs, reach, 3)
     for half in range(scen // LANES):
         sums = [inner_ref[half, number] for number in range(COUNT)]
         sums = gram(fields, coef, half, (*range(ITERS + 1), *range(rows - ITERS, rows)), own, sums)
@@ -385,7 +404,6 @@
     tall, wide = rows + 2 * HALO, cols + 4 * TILE
     coef = [resident(tall, wide, LANES)] * 4
     field = resident(halves, tall, wide, LANES)
-    scratch = [pltpu.VMEM((wide, LANES), jnp.float32)]
     params = pltpu.CompilerParams(vmem_limit_bytes=4 * MIB)
 
     def cost(microseconds):
@@ -396,37 +414,32 @@
         in_specs=[ON_CHIP] * 2,
         out_specs=[ON_CHIP] * 5,
         out_shape=coef + [field],
-        scratch_shapes=scratch,
         compiler_params=params,
         cost_estimate=cost(8),
     )(rhs, turned)
+    end = swaps(*messages(rhs, turned, *side, coefs[0]), ROW)
     partial = resident(halves, SUMS, TILE, LANES)
     *coefs, v0, v1, v2, v3, sums = pl.pallas_call(
         lambda *refs: inner_kernel(grid, *refs),
         in_specs=[ON_CHIP] * 9,
         out_specs=[ON_CHIP] * 9,
         out_shape=coef + [field] * ITERS + [partial],
-        scratch_shapes=scratch,
         input_output_aliases={4 + n: n for n in range(5)},
         compiler_params=params,
         cost_estimate=cost(14),
     )(rhs, turned, *side, *coefs, v0)
 
-    def finish(end):
-        state = [*coefs, v0, v1, v2, v3]
-        *out, total = pl.pallas_call(
-            lambda *refs: outer_kernel(grid, *refs),
-            in_specs=[ON_CHIP] * 15,
-            out_specs=[ON_CHIP] * 9,
-            out_shape=coef + [field] * ITERS + [resident(SUMS, scen)],
-            scratch_shapes=scratch,
+    state = [*coefs, v0, v1, v2, v3]
+    *out, total = pl.pallas_call(
+        lambda *refs: outer_kernel(grid, *refs),
+        in_specs=[ON_CHIP] * 15,
+        out_specs=[ON_CHIP] * 9,
+        out_shape=coef + [field] * ITERS + [resident(SUMS, scen)],
             input_output_aliases={7 + n: n for n in range(8)},
-            compiler_params=params,
-            cost_estimate=cost(7),
-        )(rhs, turned, *side, *end, sums, *state)
-        return out[4:], total
-
-    return finish
+        compiler_params=params,
+        cost_estimate=cost(7),
+    )(rhs, turned, *side, *end, sums, *state)
+    return out[4:], total
 
 
 def coefficients(moment, square):
@@ -533,8 +546,11 @@
 def sum_everywhere(value):
     for axis in ("core", "z", "y", "x"):
         count = lax.axis_size(axis)
-        for flip in (1,) if count == 2 else (1, 3):
-            value = value + lax.ppermute(value, axis, [(i, i ^ flip) for i in range(count)])
+        others = [lax.ppermute(value, axis, [(i, i ^ flip) for i in range(count)]) for flip in range(1, count)]
+        if count == 4:
+            value = (value + others[0]) + (others[1] + others[2])
+        else:
+            value = value + others[0]
     return value
 
 
@@ -543,9 +559,7 @@
     grid = (rows * lax.axis_size(ROW), cols * lax.axis_size(COL))
     rhs, turned, *side = prepare(loads, scales.T, edge_h, edge_v, pads)
     side = swaps(*side, COL)
-    finish = basis(grid, rhs, turned, side)
-    end = swaps(*messages(rhs, turned, *side), ROW)
-    fields, sums = finish(end)
+    fields, sums = basis(grid, rhs, turned, side)
     return combine(sum_everywhere(sums), fields, scen, rows, cols)
 
 

time: 92.3 us -> 67.2 us (0.73)
  Pallas kernels: 43.8 us -> 31.6 us
  local copies, waits for them, and re-layouts: 5.03 us -> 0 us
  starting transfers between devices: 26.1 us -> 22.4 us
  waiting for transfers between devices: 16 us -> 12.3 us
    pallas_call x3, Pallas kernels: 17.6 us -> 10.2 us  [the longest x1 5.98 us: basis(): pl.pallas_call(lambda *refs: outer_kernel(grid, *refs), in_specs=[ON_CHIP...]
    unnamed x10 -> x0, local copies, waits for them, and re-layouts: 5.03 us -> none
    pallas_call x1, Pallas kernels: 8.36 us -> 4.29 us  [basis(): pl.pallas_call(lambda *refs: own_kernel(grid, *refs), in_specs=[ON_CHIP]...]
    ppermute x7 -> x10, starting transfers between devices: 22.5 us -> 18.8 us  [sum_everywhere(): lax.ppermute(value, axis, [(i, i ^ flip) for i in range(count)])]
    ppermute x2, waiting for transfers between devices: 3.01 us -> 0.01 us  [swaps(): lax.ppermute(first, axes, [(i, i ^ 1) for i in range(count)])]
    ppermute x7 -> x10, waiting for transfers between devices: 13 us -> 12.3 us  [sum_everywhere(): lax.ppermute(value, axis, [(i, i ^ flip) for i in range(count)])]
  transfers between devices with their start and end apart: 11 -> 14, of which waited for: 8 -> 8; matrix products, arithmetic and copies ran while one was open for 0% -> 0% of each run, Pallas kernels for 25% -> 27%
where the time goes in v1:
time: 67.2 us; the launch traced here: 67 us
  Pallas kernels  31.6 us (47%)
  starting transfers between devices  22.4 us (33%)
  waiting for transfers between devices  12.3 us (18%)
  between operations  0.75 us (1%)
    ppermute x10, starting transfers between devices, sum_everywhere(): lax.ppermute(value, axis, [(i, i ^ flip) for i in range(count)])  18.8 us
    pallas_call x1, Pallas kernels, basis(): pl.pallas_call(lambda *refs: inner_kernel(grid, *refs), in_specs=[ON_CHIP...  13.9 us
    ppermute x10, waiting for transfers between devices, sum_everywhere(): lax.ppermute(value, axis, [(i, i ^ flip) for i in range(count)])  12.3 us
    pallas_call x1, Pallas kernels, basis(): pl.pallas_call(lambda *refs: outer_kernel(grid, *refs), in_specs=[ON_CHIP...  5.98 us
    pallas_call x1, Pallas kernels, basis(): pl.pallas_call(lambda *refs: own_kernel(grid, *refs), in_specs=[ON_CHIP]...  4.29 us
    pallas_call x1, Pallas kernels, prepare(): pl.pallas_call(prepare_kernel, in_specs=[IN_HBM] * 5, out_specs=[ON_CHIP]...  4.13 us
    pallas_call x1, Pallas kernels, combine(): pl.pallas_call(combine_kernel, in_specs=[ON_CHIP] * 5, out_specs=[IN_HBM,...  3.2 us
    ppermute x2, starting transfers between devices, swaps(): lax.ppermute(first, axes, [(i, i ^ 1) for i in range(count)])  2.17 us
  transfers between devices with their start and end apart: 14, of which 8 were waited for; matrix products, arithmetic and copies ran while one was open for 0% of the time, Pallas kernels for 27%

profile of v1, /device:TPU:0, one launch (start us, length us, event | category | flops | bytes accessed | tf_op | source)
XLA Modules:
  0.0 67.0 jit_solution(17923828993426465044)
XLA Ops:
  0.6 4.1 %shard_map.68 = (f32[32,128,256]{2,1,0:T(8,128)S(1)}, f32[128,128]{1,0:T(8,128)S(1)}, f32[17,8,256]{2,1,0:T(8,128)S(1)}, f32[17,8,256]{2,1,0:T(8,128)S(1)}) custom-call(s32[256,32,128]{2,1,0:T(8,128)} %loads_hbm.1, f32[8,256]{1,0:T(8,128)} %bitcast.2, s32[32,128]{1,0:T(8,128)} %eh_hbm.1, s32[32,128]{1,0:T(8,128)} %ev_hbm.1, s32[32,128]{1,0:T(8,128)} %pads_hbm.1), custom_call_target="tpu_custom_call" | custom-call | flops 20000000 | bytes 12582912 | tf_op jit(solution)/shard_map/pallas_call | solution.py:126
  4.8 2.1 %collective-permute-start = (f32[17,8,256]{2,1,0:T(8,128)S(1)}, f32[17,8,256]{2,1,0:T(8,128)S(1)}, u32[]{:S(2)}, u32[]{:S(2)}) collective-permute-start(f32[17,8,256]{2,1,0:T(8,128)S(1)} %get-tuple-element.31), channel_id=1, source_target_pairs={{0,1},{1,0},{2,3},{3,2},{4,5},{5,4},{6,7},{7,6},{8,9},{9,8},{10,11... | collective-permute-start | bytes 417800 | tf_op jit(solution)/shard_map/ppermute | solution.py:65
  6.9 0.7 collective-permute-start.1
  7.5 4.3 %shard_map.69 = (f32[40,160,128]{2,1,0:T(8,128)S(1)}, f32[40,160,128]{2,1,0:T(8,128)S(1)}, f32[40,160,128]{2,1,0:T(8,128)S(1)}, f32[40,160,128]{2,1,0:T(8,128)S(1)}, f32[2,40,160,128]{3,2,1,0:T(8,128)S(1)}) custom-call(f32[32,128,256]{2,1,0:T(8,128)S(1)} %get-tuple-element.29.refs_0_.rhs_ref, f32[128,128]{1,0:T(8,128)S(1)} %get-tuple-element.30.refs_1_.turned_ref), custom_call_target="tpu_custom_call" | custom-call | bytes 24000000 | tf_op jit(solution)/shard_map/pallas_call | solution.py:412
  11.8 0.0 collective-permute-done.side_a.refs_2_
  11.8 0.0 collective-permute-done.1.side_b.refs_3_
  11.8 0.1 shard_map.70
  11.9 0.1 collective-permute-start.2
  12.0 0.7 %collective-permute-start.3 = (f32[77,8,256]{2,1,0:T(8,128)S(1)}, f32[77,8,256]{2,1,0:T(8,128)S(1)}, u32[]{:S(2)}, u32[]{:S(2)}) collective-permute-start(f32[77,8,256]{2,1,0:T(8,128)S(1)} %get-tuple-element.35), channel_id=1, source_target_pairs={{16,32},{48,64},{80,96},{32,16},{64,48},{96,80},{17,33},{49,65},{8... | collective-permute-start | bytes 1892360 | tf_op jit(solution)/shard_map/ppermute | solution.py:66
  12.7 13.9 %shard_map.71 = (f32[40,160,128]{2,1,0:T(8,128)S(1)}, f32[40,160,128]{2,1,0:T(8,128)S(1)}, f32[40,160,128]{2,1,0:T(8,128)S(1)}, f32[40,160,128]{2,1,0:T(8,128)S(...) custom-call(f32[32,128,256]{2,1,0:T(8,128)S(1)} %get-tuple-element.2, ...), custom_call_target="tpu_custom_call", output_to_operand_aliasing={{0}: (4, {}), {1}: (5, {}), {2}: (6, {}), {3}: (7, {}), {4}... | custom-call | bytes 42000000 | tf_op jit(solution)/shard_map/pallas_call | solution.py:422
  26.7 0.0 collective-permute-done.2.refs_4_
  26.7 0.0 collective-permute-done.3.refs_5_
  26.7 6.0 %shard_map.72 = (f32[40,160,128]{2,1,0:T(8,128)S(1)}, f32[40,160,128]{2,1,0:T(8,128)S(1)}, f32[40,160,128]{2,1,0:T(8,128)S(1)}, f32[40,160,128]{2,1,0:T(8,128)S(...) custom-call(f32[32,128,256]{2,1,0:T(8,128)S(1)} %get-tuple-element.2, ...), custom_call_target="tpu_custom_call", output_to_operand_aliasing={{0}: (7, {}), {1}: (8, {}), {2}: (9, {}), {3}: (10, {}), {4... | custom-call | bytes 21000000 | tf_op jit(solution)/shard_map/pallas_call | solution.py:433
  32.7 2.9 %collective-permute-start.4 = (f32[24,256]{1,0:T(8,128)S(1)}, f32[24,256]{1,0:T(8,128)S(1)}, u32[]{:S(2)}, u32[]{:S(2)}) collective-permute-start(f32[24,256]{1,0:T(8,128)S(1)} %get-tuple-element.49), channel_id=1, source_target_pairs={{0,16},{16,0},{1,17},{17,1},{2,18},{18,2},{3,19},{19,3},{4,20},{20... | collective-permute-start | bytes 73736 | tf_op jit(solution)/shard_map/ppermute | solution.py:549
  35.6 0.8 %collective-permute-done.4 = f32[24,256]{1,0:T(8,128)S(1)} collective-permute-done((f32[24,256]{1,0:T(8,128)S(1)}, f32[24,256]{1,0:T(8,128)S(1)}, u32[]{:S(2)}, u32[]{:S(2)}) %collective-permute-start.4) | collective-permute-done | bytes 24608 | tf_op jit(solution)/shard_map/ppermute | solution.py:549
  36.4 6.7 %collective-permute-start.7 = (f32[24,256]{1,0:T(8,128)S(1)}, f32[24,256]{1,0:T(8,128)S(1)}, u32[]{:S(2)}, u32[]{:S(2)}) collective-permute-start(f32[24,256]{1,0:T(8,128)S(1)} %add.30), channel_id=1, source_target_pairs={{0,3},{1,2},{2,1},{3,0},{4,7},{5,6},{6,5},{7,4},{8,11},{9,10},{10,... | collective-permute-start | bytes 73736 | tf_op jit(solution)/shard_map/ppermute | solution.py:549
  43.1 0.2 collective-permute-start.6
  43.3 0.7 %collective-permute-start.5 = (f32[24,256]{1,0:T(8,128)S(1)}, f32[24,256]{1,0:T(8,128)S(1)}, u32[]{:S(2)}, u32[]{:S(2)}) collective-permute-start(f32[24,256]{1,0:T(8,128)S(1)} %add.30), channel_id=1, source_target_pairs={{0,1},{1,0},{2,3},{3,2},{4,5},{5,4},{6,7},{7,6},{8,9},{9,8},{10,11... | collective-permute-start | bytes 73736 | tf_op jit(solution)/shard_map/ppermute | solution.py:549
  44.0 0.9 %collective-permute-done.7 = f32[24,256]{1,0:T(8,128)S(1)} collective-permute-done((f32[24,256]{1,0:T(8,128)S(1)}, f32[24,256]{1,0:T(8,128)S(1)}, u32[]{:S(2)}, u32[]{:S(2)}) %collective-permute-start.7) | collective-permute-done | bytes 24608 | tf_op jit(solution)/shard_map/ppermute | solution.py:549
  44.9 3.5 %collective-permute-done.6 = f32[24,256]{1,0:T(8,128)S(1)} collective-permute-done((f32[24,256]{1,0:T(8,128)S(1)}, f32[24,256]{1,0:T(8,128)S(1)}, u32[]{:S(2)}, u32[]{:S(2)}) %collective-permute-start.6) | collective-permute-done | bytes 24608 | tf_op jit(solution)/shard_map/ppermute | solution.py:549
  48.4 0.0 collective-permute-done.5
  48.4 1.8 %collective-permute-start.10 = (f32[24,256]{1,0:T(8,128)S(1)}, f32[24,256]{1,0:T(8,128)S(1)}, u32[]{:S(2)}, u32[]{:S(2)}) collective-permute-start(f32[24,256]{1,0:T(8,128)S(1)} %add_add_fusion.2), channel_id=1, source_target_pairs={{0,12},{4,8},{8,4},{12,0},{1,13},{5,9},{9,5},{13,1},{2,14},{6,10},... | collective-permute-start | bytes 73736 | tf_op jit(solution)/shard_map/ppermute | solution.py:549
  50.2 1.9 %collective-permute-start.9 = (f32[24,256]{1,0:T(8,128)S(1)}, f32[24,256]{1,0:T(8,128)S(1)}, u32[]{:S(2)}, u32[]{:S(2)}) collective-permute-start(f32[24,256]{1,0:T(8,128)S(1)} %add_add_fusion.2), channel_id=1, source_target_pairs={{0,8},{4,12},{8,0},{12,4},{1,9},{5,13},{9,1},{13,5},{2,10},{6,14},... | collective-permute-start | bytes 73736 | tf_op jit(solution)/shard_map/ppermute | solution.py:549
  52.1 0.5 collective-permute-start.8
  52.6 0.9 %collective-permute-done.10 = f32[24,256]{1,0:T(8,128)S(1)} collective-permute-done((f32[24,256]{1,0:T(8,128)S(1)}, f32[24,256]{1,0:T(8,128)S(1)}, u32[]{:S(2)}, u32[]{:S(2)}) %collective-permute-start.10) | collective-permute-done | bytes 24608 | tf_op jit(solution)/shard_map/ppermute | solution.py:549
  53.5 2.0 %collective-permute-done.9 = f32[24,256]{1,0:T(8,128)S(1)} collective-permute-done((f32[24,256]{1,0:T(8,128)S(1)}, f32[24,256]{1,0:T(8,128)S(1)}, u32[]{:S(2)}, u32[]{:S(2)}) %collective-permute-start.9) | collective-permute-done | bytes 24608 | tf_op jit(solution)/shard_map/ppermute | solution.py:549
  55.5 0.4 collective-permute-done.8
  56.0 2.5 %collective-permute-start.13 = (f32[24,256]{1,0:T(8,128)S(1)}, f32[24,256]{1,0:T(8,128)S(1)}, u32[]{:S(2)}, u32[]{:S(2)}) collective-permute-start(f32[24,256]{1,0:T(8,128)S(1)} %add_add_fusion.1), channel_id=1, source_target_pairs={{0,96},{32,64},{64,32},{96,0},{1,97},{33,65},{65,33},{97,1},{2,98}... | collective-permute-start | bytes 73736 | tf_op jit(solution)/shard_map/ppermute | solution.py:549
  58.5 1.1 %collective-permute-start.12 = (f32[24,256]{1,0:T(8,128)S(1)}, f32[24,256]{1,0:T(8,128)S(1)}, u32[]{:S(2)}, u32[]{:S(2)}) collective-permute-start(f32[24,256]{1,0:T(8,128)S(1)} %add_add_fusion.1), channel_id=1, source_target_pairs={{0,64},{32,96},{64,0},{96,32},{1,65},{33,97},{65,1},{97,33},{2,66}... | collective-permute-start | bytes 73736 | tf_op jit(solution)/shard_map/ppermute | solution.py:549
  59.6 0.5 collective-permute-start.11
  60.2 0.9 %collective-permute-done.13 = f32[24,256]{1,0:T(8,128)S(1)} collective-permute-done((f32[24,256]{1,0:T(8,128)S(1)}, f32[24,256]{1,0:T(8,128)S(1)}, u32[]{:S(2)}, u32[]{:S(2)}) %collective-permute-start.13) | collective-permute-done | bytes 24608 | tf_op jit(solution)/shard_map/ppermute | solution.py:549
  61.1 2.7 %collective-permute-done.12 = f32[24,256]{1,0:T(8,128)S(1)} collective-permute-done((f32[24,256]{1,0:T(8,128)S(1)}, f32[24,256]{1,0:T(8,128)S(1)}, u32[]{:S(2)}, u32[]{:S(2)}) %collective-permute-start.12) | collective-permute-done | bytes 24608 | tf_op jit(solution)/shard_map/ppermute | solution.py:549
  63.8 0.0 collective-permute-done.11
  63.8 3.2 %shard_map.73 = (f32[256,32,128]{2,1,0:T(8,128)}, f32[5,256]{1,0:T(8,128)}) custom-call(f32[24,256]{1,0:T(8,128)S(1)} %add_add_fusion.sums_ref, f32[2,40,160,128]{3,2,1,0:T(8,128)S(1)} %get-tuple-element.50.v0, f32[2,40,160,128]{3,2,1,0:T(8,128)S(1)} %get-tuple-element.51.v1, f32[2,40,160,128]{3,2,1,0:T(8,128)S(1)} %get-tuple-element.52.v2, ...), custom_call_target="tpu_custom_call" | custom-call | tf_op jit(solution)/shard_map/pallas_call | solution.py:528
  (4 shorter events, 0.0 us)
Async XLA Ops:
  4.8 7.0 %collective-permute-start = (f32[17,8,256]{2,1,0:T(8,128)S(1)}, f32[17,8,256]{2,1,0:T(8,128)S(1)}, u32[]{:S(2)}, u32[]{:S(2)}) collective-permute-start(f32[17,8,256]{2,1,0:T(8,128)S(1)} %get-tuple-element.31), channel_id=1, source_target_pairs={{0,1},{1,0},{2,3},{3,2},{4,5},{5,4},{6,7},{7,6},{8,9},{9,8},{10,11... | collective-permute-start | bytes 417800 | tf_op jit(solution)/shard_map/ppermute | solution.py:65
  6.9 5.0 %collective-permute-start.1 = (f32[17,8,256]{2,1,0:T(8,128)S(1)}, f32[17,8,256]{2,1,0:T(8,128)S(1)}, u32[]{:S(2)}, u32[]{:S(2)}) collective-permute-start(f32[17,8,256]{2,1,0:T(8,128)S(1)} %get-tuple-element.32), channel_id=1, source_target_pairs={{1,2},{3,4},{5,6},{7,8},{9,10},{11,12},{13,14},{2,1},{4,3},{6,5},{... | collective-permute-start | bytes 417800 | tf_op jit(solution)/shard_map/ppermute | solution.py:66
  11.9 14.7 %collective-permute-start.2 = (f32[77,8,256]{2,1,0:T(8,128)S(1)}, f32[77,8,256]{2,1,0:T(8,128)S(1)}, u32[]{:S(2)}, u32[]{:S(2)}) collective-permute-start(f32[77,8,256]{2,1,0:T(8,128)S(1)} %get-tuple-element.34), channel_id=1, source_target_pairs={{0,16},{16,0},{32,48},{48,32},{64,80},{80,64},{96,112},{112,96},{1... | collective-permute-start | bytes 1892360 | tf_op jit(solution)/shard_map/ppermute | solution.py:65
  12.0 14.6 %collective-permute-start.3 = (f32[77,8,256]{2,1,0:T(8,128)S(1)}, f32[77,8,256]{2,1,0:T(8,128)S(1)}, u32[]{:S(2)}, u32[]{:S(2)}) collective-permute-start(f32[77,8,256]{2,1,0:T(8,128)S(1)} %get-tuple-element.35), channel_id=1, source_target_pairs={{16,32},{48,64},{80,96},{32,16},{64,48},{96,80},{17,33},{49,65},{8... | collective-permute-start | bytes 1892360 | tf_op jit(solution)/shard_map/ppermute | solution.py:66
  32.7 3.7 %collective-permute-start.4 = (f32[24,256]{1,0:T(8,128)S(1)}, f32[24,256]{1,0:T(8,128)S(1)}, u32[]{:S(2)}, u32[]{:S(2)}) collective-permute-start(f32[24,256]{1,0:T(8,128)S(1)} %get-tuple-element.49), channel_id=1, source_target_pairs={{0,16},{16,0},{1,17},{17,1},{2,18},{18,2},{3,19},{19,3},{4,20},{20... | collective-permute-start | bytes 73736 | tf_op jit(solution)/shard_map/ppermute | solution.py:549
  36.4 8.5 %collective-permute-start.7 = (f32[24,256]{1,0:T(8,128)S(1)}, f32[24,256]{1,0:T(8,128)S(1)}, u32[]{:S(2)}, u32[]{:S(2)}) collective-permute-start(f32[24,256]{1,0:T(8,128)S(1)} %add.30), channel_id=1, source_target_pairs={{0,3},{1,2},{2,1},{3,0},{4,7},{5,6},{6,5},{7,4},{8,11},{9,10},{10,... | collective-permute-start | bytes 73736 | tf_op jit(solution)/shard_map/ppermute | solution.py:549
  43.1 5.3 %collective-permute-start.6 = (f32[24,256]{1,0:T(8,128)S(1)}, f32[24,256]{1,0:T(8,128)S(1)}, u32[]{:S(2)}, u32[]{:S(2)}) collective-permute-start(f32[24,256]{1,0:T(8,128)S(1)} %add.30), channel_id=1, source_target_pairs={{0,2},{1,3},{2,0},{3,1},{4,6},{5,7},{6,4},{7,5},{8,10},{9,11},{10,... | collective-permute-start | bytes 73736 | tf_op jit(solution)/shard_map/ppermute | solution.py:549
  43.3 5.1 %collective-permute-start.5 = (f32[24,256]{1,0:T(8,128)S(1)}, f32[24,256]{1,0:T(8,128)S(1)}, u32[]{:S(2)}, u32[]{:S(2)}) collective-permute-start(f32[24,256]{1,0:T(8,128)S(1)} %add.30), channel_id=1, source_target_pairs={{0,1},{1,0},{2,3},{3,2},{4,5},{5,4},{6,7},{7,6},{8,9},{9,8},{10,11... | collective-permute-start | bytes 73736 | tf_op jit(solution)/shard_map/ppermute | solution.py:549
  48.4 5.1 %collective-permute-start.10 = (f32[24,256]{1,0:T(8,128)S(1)}, f32[24,256]{1,0:T(8,128)S(1)}, u32[]{:S(2)}, u32[]{:S(2)}) collective-permute-start(f32[24,256]{1,0:T(8,128)S(1)} %add_add_fusion.2), channel_id=1, source_target_pairs={{0,12},{4,8},{8,4},{12,0},{1,13},{5,9},{9,5},{13,1},{2,14},{6,10},... | collective-permute-start | bytes 73736 | tf_op jit(solution)/shard_map/ppermute | solution.py:549
  50.2 5.3 %collective-permute-start.9 = (f32[24,256]{1,0:T(8,128)S(1)}, f32[24,256]{1,0:T(8,128)S(1)}, u32[]{:S(2)}, u32[]{:S(2)}) collective-permute-start(f32[24,256]{1,0:T(8,128)S(1)} %add_add_fusion.2), channel_id=1, source_target_pairs={{0,8},{4,12},{8,0},{12,4},{1,9},{5,13},{9,1},{13,5},{2,10},{6,14},... | collective-permute-start | bytes 73736 | tf_op jit(solution)/shard_map/ppermute | solution.py:549
  52.1 3.8 %collective-permute-start.8 = (f32[24,256]{1,0:T(8,128)S(1)}, f32[24,256]{1,0:T(8,128)S(1)}, u32[]{:S(2)}, u32[]{:S(2)}) collective-permute-start(f32[24,256]{1,0:T(8,128)S(1)} %add_add_fusion.2), channel_id=1, source_target_pairs={{0,4},{4,0},{8,12},{12,8},{1,5},{5,1},{9,13},{13,9},{2,6},{6,2},{1... | collective-permute-start | bytes 73736 | tf_op jit(solution)/shard_map/ppermute | solution.py:549
  56.0 5.1 %collective-permute-start.13 = (f32[24,256]{1,0:T(8,128)S(1)}, f32[24,256]{1,0:T(8,128)S(1)}, u32[]{:S(2)}, u32[]{:S(2)}) collective-permute-start(f32[24,256]{1,0:T(8,128)S(1)} %add_add_fusion.1), channel_id=1, source_target_pairs={{0,96},{32,64},{64,32},{96,0},{1,97},{33,65},{65,33},{97,1},{2,98}... | collective-permute-start | bytes 73736 | tf_op jit(solution)/shard_map/ppermute | solution.py:549
  58.5 5.3 %collective-permute-start.12 = (f32[24,256]{1,0:T(8,128)S(1)}, f32[24,256]{1,0:T(8,128)S(1)}, u32[]{:S(2)}, u32[]{:S(2)}) collective-permute-start(f32[24,256]{1,0:T(8,128)S(1)} %add_add_fusion.1), channel_id=1, source_target_pairs={{0,64},{32,96},{64,0},{96,32},{1,65},{33,97},{65,1},{97,33},{2,66}... | collective-permute-start | bytes 73736 | tf_op jit(solution)/shard_map/ppermute | solution.py:549
  59.6 4.2 %collective-permute-start.11 = (f32[24,256]{1,0:T(8,128)S(1)}, f32[24,256]{1,0:T(8,128)S(1)}, u32[]{:S(2)}, u32[]{:S(2)}) collective-permute-start(f32[24,256]{1,0:T(8,128)S(1)} %add_add_fusion.1), channel_id=1, source_target_pairs={{0,32},{32,0},{64,96},{96,64},{1,33},{33,1},{65,97},{97,65},{2,34}... | collective-permute-start | bytes 73736 | tf_op jit(solution)/shard_map/ppermute | solution.py:549

commit v2 on v1

--- a/solution.py
+++ b/solution.py
@@ -1,7 +1,10 @@
+import functools
+
 import jax
 import jax.numpy as jnp
 from jax import lax
 from jax.experimental import pallas as pl
+from jax.experimental.layout import Layout, with_layout_constraint
 from jax.experimental.pallas import tpu as pltpu
 from jax.sharding import Mesh
 from jax.sharding import PartitionSpec as P
@@ -22,6 +25,8 @@
 LEFT = TILE
 COUNT = 2 * ITERS + (ITERS + 1) * (ITERS + 2) // 2
 SUMS = 24
+PRODUCT_LOSS = 4000.0
+NORM_LOSS = 8000.0
 MIB = 1024 * 1024
 ON_CHIP = pl.BlockSpec(memory_space=pltpu.VMEM)
 IN_HBM = pl.BlockSpec(memory_space=pltpu.HBM)
@@ -445,26 +450,35 @@
 def coefficients(moment, square):
     count = ITERS + 1
 
+    worst = [jnp.zeros_like(moment[0])]
+
+    def add(terms):
+        total, size = terms[0], jnp.abs(terms[0])
+        for term in terms[1:]:
+            total, size = total + term, size + jnp.abs(term)
+        return total, size
+
     def product(left, right):
         powers = {}
         for i, a in left.items():
             for j, b in right.items():
                 powers[i + j] = powers[i + j] + a * b if i + j in powers else a * b
-        total = None
-        for power, value in powers.items():
-            term = value * moment[power]
-            total = term if total is None else total + term
+        total, size = add([value * moment[power] for power, value in powers.items()])
+        worst.append(jnp.where(size <= PRODUCT_LOSS * total, 0.0, 1.0))
         return total
 
     def norm(resid):
-        total = None
+        terms = []
         for i in range(count):
             for j in range(i, count):
                 if i in resid and j in resid:
                     term = resid[i] * resid[j] * square[i, j]
-                    term = term if i == j else 2.0 * term
-                    total = term if total is None else total + term
-        return jnp.sqrt(jnp.maximum(total, 0.0))
+                    terms.append(term if i == j else 2.0 * term)
+        total, size = add(terms)
+        value = jnp.sqrt(jnp.maximum(total, 0.0))
+        scale = functools.reduce(jnp.maximum, norms + [value])
+        worst.append(jnp.where(size <= NORM_LOSS * scale * jnp.maximum(value, 1e-4 * jnp.sqrt(size)), 0.0, 1.0))
+        return value
 
     def plus(left, factor, right):
         out = dict(left)
@@ -488,10 +502,10 @@
             gamma_new = product(resid, resid)
             direction = plus(resid, gamma_new / gamma, direction)
             gamma = gamma_new
-    return [solution[i] for i in range(ITERS)], norms
-
-
-def combine_kernel(sums_ref, v0, v1, v2, v3, out_hbm, norms_ref, factor_ref, buf, sem):
+    return [solution[i] for i in range(ITERS)], norms, functools.reduce(jnp.maximum, worst)
+
+
+def combine_kernel(sums_ref, v0, v1, v2, v3, out_hbm, norms_ref, doubt_ref, factor_ref, buf, sem):
     scen, rows, cols = out_hbm.shape
     line = lambda n: sums_ref[n : n + 1, :]
     moment = [line(n) for n in range(2 * ITERS)]
@@ -500,7 +514,8 @@
         for j in range(i, ITERS + 1):
             square[i, j] = line(number)
             number += 1
-    factors, norms = coefficients(moment, square)
+    factors, norms, doubt = coefficients(moment, square)
+    doubt_ref[0] = jnp.max(doubt).astype(jnp.int32)
     for number, value in enumerate(factors):
         factor_ref[number : number + 1, :] = value
     for number, value in enumerate(norms):
@@ -525,13 +540,14 @@
 
 
 def combine(sums, fields, scen, rows, cols):
-    drop, norms = pl.pallas_call(
+    drop, norms, doubt = pl.pallas_call(
         combine_kernel,
         in_specs=[ON_CHIP] * 5,
-        out_specs=[IN_HBM, ON_CHIP],
+        out_specs=[IN_HBM, ON_CHIP, pl.BlockSpec(memory_space=pltpu.SMEM)],
         out_shape=[
-            jax.ShapeDtypeStruct((scen, rows, cols), jnp.float32),
+            pltpu.HBM((scen, rows, cols), jnp.float32),
             jax.ShapeDtypeStruct((ITERS + 1, scen), jnp.float32),
+            jax.ShapeDtypeStruct((1,), jnp.int32),
         ],
         scratch_shapes=[
             pltpu.VMEM((TILE, scen), jnp.float32),
@@ -540,7 +556,7 @@
         ],
         compiler_params=pltpu.CompilerParams(vmem_limit_bytes=8 * MIB),
     )(sums, *fields)
-    return drop, norms.T
+    return drop, norms, doubt[0]
 
 
 def sum_everywhere(value):
@@ -554,13 +570,102 @@
     return value
 
 
+def padded_2(shard, sides, width):
+    edges = {}
+    for axis, dim in sides:
+        devices, length = (lax.axis_size(axis), shard.shape[dim])
+        up = [(i, (i + 1) % devices) for i in range(devices - 1)]
+        last = lax.slice_in_dim(shard, length - width, length, axis=dim)
+        leading = lax.slice_in_dim(shard, 0, width, axis=dim)
+        edges[dim] = (
+            lax.ppermute(last, axis, up),
+            lax.ppermute(leading, axis, [(b, a) for a, b in up]),
+        )
+    done = []
+    for _, dim in sides:
+        low, high = edges[dim]
+        around = [(width, width) if d in done else (0, 0) for d in range(shard.ndim)]
+        shard = jnp.concatenate([jnp.pad(low, around), shard, jnp.pad(high, around)], axis=dim)
+        done.append(dim)
+    return shard
+
+
+def passed_along(value, axis, steps):
+    count = lax.axis_size(axis)
+    leading, last = (max(0, -steps), min(count, count - steps))
+    return lax.ppermute(value, axis, [(source, source + steps) for source in range(leading, last)])
+
+
+def apply_grid(field, g_east, g_west, g_south, g_north, diagonal):
+    padded = padded_2(field, ((ROW, 1), (COL, 2)), 1)
+    north = padded[:, :-2, 1:-1]
+    south = padded[:, 2:, 1:-1]
+    west = padded[:, 1:-1, :-2]
+    east = padded[:, 1:-1, 2:]
+    return diagonal * field - (g_east * east + g_west * west + g_south * south + g_north * north)
+
+
+def inner(left, right):
+    return jnp.sum(left * right, axis=(1, 2))
+
+
+def recurrence(edge_h, edge_v, pads, loads, scales):
+    rows, cols = pads.shape
+    row_ids = lax.axis_index(ROW) * rows + lax.broadcasted_iota(jnp.int32, (rows, cols), 0)
+    col_ids = lax.axis_index(COL) * cols + lax.broadcasted_iota(jnp.int32, (rows, cols), 1)
+    zero = jnp.zeros((rows, cols), jnp.float32)
+    g_east = jnp.where(col_ids < cols * lax.axis_size(COL) - 1, lookup(edge_h, edge_table), zero)
+    g_south = jnp.where(row_ids < rows * lax.axis_size(ROW) - 1, lookup(edge_v, edge_table), zero)
+    west_rim = passed_along(g_east[:, cols - 1 :], COL, 1)
+    north_rim = passed_along(g_south[rows - 1 :, :], ROW, 1)
+    g_west = jnp.concatenate([west_rim, g_east[:, : cols - 1]], axis=1)
+    g_north = jnp.concatenate([north_rim, g_south[: rows - 1]], axis=0)
+    diagonal = (
+        g_east + g_west + g_south + g_north + pads.astype(jnp.float32) * pad_conductance + leakage
+    )
+    weights = -scales * jnp.asarray(load_table, jnp.float32)[None, :]
+    right = jnp.zeros(loads.shape, jnp.float32)
+    for number in range(8):
+        right = right + jnp.where(
+            loads == number, weights[:, number][:, None, None], jnp.float32(0.0)
+        )
+
+    def operate(field):
+        return apply_grid(field, g_east, g_west, g_south, g_north, diagonal)
+
+    def iterate(number, carry):
+        solution, resid, direction, gamma, norms = carry
+        image = operate(direction)
+        alpha = gamma / sum_everywhere(inner(direction, image))
+        solution = solution + alpha[:, None, None] * direction
+        resid = resid - alpha[:, None, None] * image
+        precond = resid / diagonal
+        gamma_new, squares = sum_everywhere(jnp.stack([inner(resid, precond), inner(resid, resid)]))
+        norms = lax.dynamic_update_slice(norms, jnp.sqrt(squares)[None], (number + 1, 0))
+        direction = precond + (gamma_new / gamma)[:, None, None] * direction
+        return solution, resid, direction, gamma_new, norms
+
+    precond = right / diagonal
+    gamma, squares = sum_everywhere(jnp.stack([inner(right, precond), inner(right, right)]))
+    norms = jnp.zeros((ITERS + 1, squares.shape[0]), jnp.float32).at[0].set(jnp.sqrt(squares))
+    carry = (jnp.zeros_like(right), right, precond, gamma, norms)
+    solution, _, _, _, norms = lax.fori_loop(0, ITERS, iterate, carry)
+    return solution, norms
+
+
 def local(edge_h, edge_v, pads, loads, scales):
     scen, rows, cols = loads.shape
     grid = (rows * lax.axis_size(ROW), cols * lax.axis_size(COL))
     rhs, turned, *side = prepare(loads, scales.T, edge_h, edge_v, pads)
     side = swaps(*side, COL)
     fields, sums = basis(grid, rhs, turned, side)
-    return combine(sum_everywhere(sums), fields, scen, rows, cols)
+    drop, norms, doubt = combine(sum_everywhere(sums), fields, scen, rows, cols)
+    def again(drop, norms):
+        drop, norms = recurrence(edge_h, edge_v, pads, loads, scales)
+        return with_layout_constraint(drop, Layout((0, 1, 2))), norms
+
+    drop, norms = lax.cond(doubt > 0, again, lambda drop, norms: (drop, norms), drop, norms)
+    return drop, norms.T
 
 
 def solution(mesh):

time: 67.2 us -> 72.2 us (1.074)
  starting transfers between devices: 22.4 us -> 24 us
  waiting for transfers between devices: 12.3 us -> 13.7 us
  between operations: 0.75 us -> 1.55 us
  Pallas kernels: 31.6 us -> 32.4 us
    ppermute x10, starting transfers between devices: 18.8 us -> 20.5 us  [sum_everywhere(): lax.ppermute(value, axis, [(i, i ^ flip) for i in range(count)])]
    ppermute x10, waiting for transfers between devices: 12.3 us -> 13.7 us  [sum_everywhere(): lax.ppermute(value, axis, [(i, i ^ flip) for i in range(count)])]
  transfers between devices with their start and end apart: 14 -> 14, of which waited for: 8 -> 7; matrix products, arithmetic and copies ran while one was open for 0% -> 0% of each run, Pallas kernels for 27% -> 26%
where the time goes in v2:
time: 72.2 us; the launch traced here: 72 us
  Pallas kernels  32.4 us (45%)
  starting transfers between devices  24 us (33%)
  waiting for transfers between devices  13.7 us (19%)
  between operations  1.55 us (2%)
    ppermute x10, starting transfers between devices, sum_everywhere(): lax.ppermute(value, axis, [(i, i ^ flip) for i in range(count)])  20.5 us
    pallas_call x1, Pallas kernels, basis(): pl.pallas_call(lambda *refs: inner_kernel(grid, *refs), in_specs=[ON_CHIP...  14.4 us
    ppermute x10, waiting for transfers between devices, sum_everywhere(): lax.ppermute(value, axis, [(i, i ^ flip) for i in range(count)])  13.7 us
    pallas_call x1, Pallas kernels, basis(): pl.pallas_call(lambda *refs: outer_kernel(grid, *refs), in_specs=[ON_CHIP...  6.28 us
    pallas_call x1, Pallas kernels, basis(): pl.pallas_call(lambda *refs: own_kernel(grid, *refs), in_specs=[ON_CHIP]...  4.35 us
    pallas_call x1, Pallas kernels, prepare(): pl.pallas_call(prepare_kernel, in_specs=[IN_HBM] * 5, out_specs=[ON_CHIP]...  4.14 us
    pallas_call x1, Pallas kernels, combine(): pl.pallas_call(combine_kernel, in_specs=[ON_CHIP] * 5, out_specs=[IN_HBM,...  3.17 us
    ppermute x2, starting transfers between devices, swaps(): lax.ppermute(first, axes, [(i, i ^ 1) for i in range(count)])  2.17 us
  transfers between devices with their start and end apart: 14, of which 7 were waited for; matrix products, arithmetic and copies ran while one was open for 0% of the time, Pallas kernels for 26%

profile of v2, /device:TPU:0, one launch (start us, length us, event | category | flops | bytes accessed | tf_op | source)
XLA Modules:
  0.0 72.0 jit_solution(10561327366202760841)
XLA Ops:
  0.6 4.1 %shard_map.78 = (f32[32,128,256]{2,1,0:T(8,128)S(1)}, f32[128,128]{1,0:T(8,128)S(1)}, f32[17,8,256]{2,1,0:T(8,128)S(1)}, f32[17,8,256]{2,1,0:T(8,128)S(1)}) custom-call(s32[256,32,128]{2,1,0:T(8,128)} %loads_hbm.1, f32[8,256]{1,0:T(8,128)} %bitcast.36, s32[32,128]{1,0:T(8,128)} %eh_hbm.1, s32[32,128]{1,0:T(8,128)} %ev_hbm.1, s32[32,128]{1,0:T(8,128)} %pads_hbm.1), custom_call_target="tpu_custom_call" | custom-call | flops 20000000 | bytes 12582912 | tf_op jit(solution)/shard_map/pallas_call | solution.py:131
  4.8 2.1 %collective-permute-start.36 = (f32[17,8,256]{2,1,0:T(8,128)S(1)}, f32[17,8,256]{2,1,0:T(8,128)S(1)}, u32[]{:S(2)}, u32[]{:S(2)}) collective-permute-start(f32[17,8,256]{2,1,0:T(8,128)S(1)} %get-tuple-element.334), channel_id=1, source_target_pairs={{0,1},{1,0},{2,3},{3,2},{4,5},{5,4},{6,7},{7,6},{8,9},{9,8},{10,11... | collective-permute-start | bytes 417800 | tf_op jit(solution)/shard_map/ppermute | solution.py:70
  6.9 0.7 collective-permute-start.37
  7.5 4.4 %shard_map.79 = (f32[40,160,128]{2,1,0:T(8,128)S(1)}, f32[40,160,128]{2,1,0:T(8,128)S(1)}, f32[40,160,128]{2,1,0:T(8,128)S(1)}, f32[40,160,128]{2,1,0:T(8,128)S(1)}, f32[2,40,160,128]{3,2,1,0:T(8,128)S(1)}) custom-call(f32[32,128,256]{2,1,0:T(8,128)S(1)} %get-tuple-element.332.refs_0_.rhs_ref, f32[128,128]{1,0:T(8,128)S(1)} %get-tuple-element.333.refs_1_.turned_ref), custom_call_target="tpu_custom_call" | custom-call | bytes 24000000 | tf_op jit(solution)/shard_map/pallas_call | solution.py:417
  11.9 0.0 collective-permute-done.36.side_a.refs_2_
  11.9 0.0 collective-permute-done.37.side_b.refs_3_
  11.9 0.1 shard_map.80
  12.0 0.1 collective-permute-start.38
  12.1 0.7 collective-permute-start.39
  12.8 14.4 %shard_map.81 = (f32[40,160,128]{2,1,0:T(8,128)S(1)}, f32[40,160,128]{2,1,0:T(8,128)S(1)}, f32[40,160,128]{2,1,0:T(8,128)S(1)}, f32[40,160,128]{2,1,0:T(8,128)S(...) custom-call(f32[32,128,256]{2,1,0:T(8,128)S(1)} %get-tuple-element.3, ...), custom_call_target="tpu_custom_call", output_to_operand_aliasing={{0}: (4, {}), {1}: (5, {}), {2}: (6, {}), {3}: (7, {}), {4}... | custom-call | bytes 42000000 | tf_op jit(solution)/shard_map/pallas_call | solution.py:427
  27.2 0.0 collective-permute-done.38.refs_4_
  27.2 0.0 collective-permute-done.39.refs_5_
  27.2 6.3 %shard_map.82 = (f32[40,160,128]{2,1,0:T(8,128)S(1)}, f32[40,160,128]{2,1,0:T(8,128)S(1)}, f32[40,160,128]{2,1,0:T(8,128)S(1)}, f32[40,160,128]{2,1,0:T(8,128)S(...) custom-call(f32[32,128,256]{2,1,0:T(8,128)S(1)} %get-tuple-element.3, ...), custom_call_target="tpu_custom_call", output_to_operand_aliasing={{0}: (7, {}), {1}: (8, {}), {2}: (9, {}), {3}: (10, {}), {4... | custom-call | bytes 21000000 | tf_op jit(solution)/shard_map/pallas_call | solution.py:438
  33.5 2.9 %collective-permute-start.40 = (f32[24,256]{1,0:T(8,128)S(1)}, f32[24,256]{1,0:T(8,128)S(1)}, u32[]{:S(2)}, u32[]{:S(2)}) collective-permute-start(f32[24,256]{1,0:T(8,128)S(1)} %get-tuple-element.352), channel_id=1, source_target_pairs={{0,16},{16,0},{1,17},{17,1},{2,18},{18,2},{3,19},{19,3},{4,20},{20... | collective-permute-start | bytes 73736 | tf_op jit(solution)/shard_map/ppermute | solution.py:565
  36.4 0.8 %collective-permute-done.40 = f32[24,256]{1,0:T(8,128)S(1)} collective-permute-done((f32[24,256]{1,0:T(8,128)S(1)}, f32[24,256]{1,0:T(8,128)S(1)}, u32[]{:S(2)}, u32[]{:S(2)}) %collective-permute-start.40) | collective-permute-done | bytes 24608 | tf_op jit(solution)/shard_map/ppermute | solution.py:565
  37.3 4.8 %collective-permute-start.41 = (f32[24,256]{1,0:T(8,128)S(1)}, f32[24,256]{1,0:T(8,128)S(1)}, u32[]{:S(2)}, u32[]{:S(2)}) collective-permute-start(f32[24,256]{1,0:T(8,128)S(1)} %add.458), channel_id=1, source_target_pairs={{0,1},{1,0},{2,3},{3,2},{4,5},{5,4},{6,7},{7,6},{8,9},{9,8},{10,11... | collective-permute-start | bytes 73736 | tf_op jit(solution)/shard_map/ppermute | solution.py:565
  42.0 3.3 %collective-permute-start.42 = (f32[24,256]{1,0:T(8,128)S(1)}, f32[24,256]{1,0:T(8,128)S(1)}, u32[]{:S(2)}, u32[]{:S(2)}) collective-permute-start(f32[24,256]{1,0:T(8,128)S(1)} %add.458), channel_id=1, source_target_pairs={{0,2},{1,3},{2,0},{3,1},{4,6},{5,7},{6,4},{7,5},{8,10},{9,11},{10,... | collective-permute-start | bytes 73736 | tf_op jit(solution)/shard_map/ppermute | solution.py:565
  45.3 0.0 collective-permute-start.43
  45.3 0.0 collective-permute-done.41
  45.3 2.1 %collective-permute-done.42 = f32[24,256]{1,0:T(8,128)S(1)} collective-permute-done((f32[24,256]{1,0:T(8,128)S(1)}, f32[24,256]{1,0:T(8,128)S(1)}, u32[]{:S(2)}, u32[]{:S(2)}) %collective-permute-start.42) | collective-permute-done | bytes 24608 | tf_op jit(solution)/shard_map/ppermute | solution.py:565
  47.4 3.0 %collective-permute-done.43 = f32[24,256]{1,0:T(8,128)S(1)} collective-permute-done((f32[24,256]{1,0:T(8,128)S(1)}, f32[24,256]{1,0:T(8,128)S(1)}, u32[]{:S(2)}, u32[]{:S(2)}) %collective-permute-start.43) | collective-permute-done | bytes 24608 | tf_op jit(solution)/shard_map/ppermute | solution.py:565
  50.4 1.7 %collective-permute-start.44 = (f32[24,256]{1,0:T(8,128)S(1)}, f32[24,256]{1,0:T(8,128)S(1)}, u32[]{:S(2)}, u32[]{:S(2)}) collective-permute-start(f32[24,256]{1,0:T(8,128)S(1)} %add_add_fusion.11), channel_id=1, source_target_pairs={{0,4},{4,0},{8,12},{12,8},{1,5},{5,1},{9,13},{13,9},{2,6},{6,2},{1... | collective-permute-start | bytes 73736 | tf_op jit(solution)/shard_map/ppermute | solution.py:565
  52.0 1.7 %collective-permute-start.45 = (f32[24,256]{1,0:T(8,128)S(1)}, f32[24,256]{1,0:T(8,128)S(1)}, u32[]{:S(2)}, u32[]{:S(2)}) collective-permute-start(f32[24,256]{1,0:T(8,128)S(1)} %add_add_fusion.11), channel_id=1, source_target_pairs={{0,8},{4,12},{8,0},{12,4},{1,9},{5,13},{9,1},{13,5},{2,10},{6,14},... | collective-permute-start | bytes 73736 | tf_op jit(solution)/shard_map/ppermute | solution.py:565
  53.7 1.4 %collective-permute-start.46 = (f32[24,256]{1,0:T(8,128)S(1)}, f32[24,256]{1,0:T(8,128)S(1)}, u32[]{:S(2)}, u32[]{:S(2)}) collective-permute-start(f32[24,256]{1,0:T(8,128)S(1)} %add_add_fusion.11), channel_id=1, source_target_pairs={{0,12},{4,8},{8,4},{12,0},{1,13},{5,9},{9,5},{13,1},{2,14},{6,10},... | collective-permute-start | bytes 73736 | tf_op jit(solution)/shard_map/ppermute | solution.py:565
  55.1 0.0 collective-permute-done.44
  55.2 2.2 %collective-permute-done.45 = f32[24,256]{1,0:T(8,128)S(1)} collective-permute-done((f32[24,256]{1,0:T(8,128)S(1)}, f32[24,256]{1,0:T(8,128)S(1)}, u32[]{:S(2)}, u32[]{:S(2)}) %collective-permute-start.45) | collective-permute-done | bytes 24608 | tf_op jit(solution)/shard_map/ppermute | solution.py:565
  57.4 1.4 %collective-permute-done.46 = f32[24,256]{1,0:T(8,128)S(1)} collective-permute-done((f32[24,256]{1,0:T(8,128)S(1)}, f32[24,256]{1,0:T(8,128)S(1)}, u32[]{:S(2)}, u32[]{:S(2)}) %collective-permute-start.46) | collective-permute-done | bytes 24608 | tf_op jit(solution)/shard_map/ppermute | solution.py:565
  58.8 1.6 %collective-permute-start.47 = (f32[24,256]{1,0:T(8,128)S(1)}, f32[24,256]{1,0:T(8,128)S(1)}, u32[]{:S(2)}, u32[]{:S(2)}) collective-permute-start(f32[24,256]{1,0:T(8,128)S(1)} %add_add_fusion.10), channel_id=1, source_target_pairs={{0,32},{32,0},{64,96},{96,64},{1,33},{33,1},{65,97},{97,65},{2,34}... | collective-permute-start | bytes 73736 | tf_op jit(solution)/shard_map/ppermute | solution.py:565
  60.4 2.4 %collective-permute-start.48 = (f32[24,256]{1,0:T(8,128)S(1)}, f32[24,256]{1,0:T(8,128)S(1)}, u32[]{:S(2)}, u32[]{:S(2)}) collective-permute-start(f32[24,256]{1,0:T(8,128)S(1)} %add_add_fusion.10), channel_id=1, source_target_pairs={{0,64},{32,96},{64,0},{96,32},{1,65},{33,97},{65,1},{97,33},{2,66}... | collective-permute-start | bytes 73736 | tf_op jit(solution)/shard_map/ppermute | solution.py:565
  62.7 0.8 %collective-permute-start.49 = (f32[24,256]{1,0:T(8,128)S(1)}, f32[24,256]{1,0:T(8,128)S(1)}, u32[]{:S(2)}, u32[]{:S(2)}) collective-permute-start(f32[24,256]{1,0:T(8,128)S(1)} %add_add_fusion.10), channel_id=1, source_target_pairs={{0,96},{32,64},{64,32},{96,0},{1,97},{33,65},{65,33},{97,1},{2,98}... | collective-permute-start | bytes 73736 | tf_op jit(solution)/shard_map/ppermute | solution.py:565
  63.6 0.0 collective-permute-done.47
  63.6 2.1 %collective-permute-done.48 = f32[24,256]{1,0:T(8,128)S(1)} collective-permute-done((f32[24,256]{1,0:T(8,128)S(1)}, f32[24,256]{1,0:T(8,128)S(1)}, u32[]{:S(2)}, u32[]{:S(2)}) %collective-permute-start.48) | collective-permute-done | bytes 24608 | tf_op jit(solution)/shard_map/ppermute | solution.py:565
  65.7 2.1 %collective-permute-done.49 = f32[24,256]{1,0:T(8,128)S(1)} collective-permute-done((f32[24,256]{1,0:T(8,128)S(1)}, f32[24,256]{1,0:T(8,128)S(1)}, u32[]{:S(2)}, u32[]{:S(2)}) %collective-permute-start.49) | collective-permute-done | bytes 24608 | tf_op jit(solution)/shard_map/ppermute | solution.py:565
  67.8 0.0 copy-start.6
  67.8 0.0 copy-start.7
  67.8 0.0 copy-start.8
  67.8 0.0 copy-start.9
  67.8 3.2 %shard_map.83 = (f32[256,32,128]{2,1,0:T(8,128)}, f32[5,256]{1,0:T(8,128)}, s32[1]{0:T(128)}) custom-call(f32[24,256]{1,0:T(8,128)S(1)} %add_add_fusion.9.sums_ref, f32[2,40,160,128]{3,2,1,0:T(8,128)S(1)} %get-tuple-element.353.v0, f32[2,40,160,128]{3,2,1,0:T(8,128)S(1)} %get-tuple-element.354.v1, f32[2,40,160,128]{3,2,1,0:T(8,128)S(1)} %get-tuple-element.355.v2, ...), custom_call_target="tpu_custom_call" | custom-call | tf_op jit(solution)/shard_map/pallas_call | solution.py:543
  71.6 0.0 copy-done.6
  71.6 0.0 copy-done.7
  71.6 0.0 copy-done.8
  71.6 0.0 copy-done.9
  71.6 0.2 conditional.1
  (4 shorter events, 0.0 us)
Async XLA Ops:
  4.8 7.1 %collective-permute-start.36 = (f32[17,8,256]{2,1,0:T(8,128)S(1)}, f32[17,8,256]{2,1,0:T(8,128)S(1)}, u32[]{:S(2)}, u32[]{:S(2)}) collective-permute-start(f32[17,8,256]{2,1,0:T(8,128)S(1)} %get-tuple-element.334), channel_id=1, source_target_pairs={{0,1},{1,0},{2,3},{3,2},{4,5},{5,4},{6,7},{7,6},{8,9},{9,8},{10,11... | collective-permute-start | bytes 417800 | tf_op jit(solution)/shard_map/ppermute | solution.py:70
  6.9 5.0 %collective-permute-start.37 = (f32[17,8,256]{2,1,0:T(8,128)S(1)}, f32[17,8,256]{2,1,0:T(8,128)S(1)}, u32[]{:S(2)}, u32[]{:S(2)}) collective-permute-start(f32[17,8,256]{2,1,0:T(8,128)S(1)} %get-tuple-element.335), channel_id=1, source_target_pairs={{1,2},{3,4},{5,6},{7,8},{9,10},{11,12},{13,14},{2,1},{4,3},{6,5},{... | collective-permute-start | bytes 417800 | tf_op jit(solution)/shard_map/ppermute | solution.py:71
  12.0 15.2 %collective-permute-start.38 = (f32[77,8,256]{2,1,0:T(8,128)S(1)}, f32[77,8,256]{2,1,0:T(8,128)S(1)}, u32[]{:S(2)}, u32[]{:S(2)}) collective-permute-start(f32[77,8,256]{2,1,0:T(8,128)S(1)} %get-tuple-element.337), channel_id=1, source_target_pairs={{0,16},{16,0},{32,48},{48,32},{64,80},{80,64},{96,112},{112,96},{1... | collective-permute-start | bytes 1892360 | tf_op jit(solution)/shard_map/ppermute | solution.py:70
  12.1 15.1 %collective-permute-start.39 = (f32[77,8,256]{2,1,0:T(8,128)S(1)}, f32[77,8,256]{2,1,0:T(8,128)S(1)}, u32[]{:S(2)}, u32[]{:S(2)}) collective-permute-start(f32[77,8,256]{2,1,0:T(8,128)S(1)} %get-tuple-element.338), channel_id=1, source_target_pairs={{16,32},{48,64},{80,96},{32,16},{64,48},{96,80},{17,33},{49,65},{8... | collective-permute-start | bytes 1892360 | tf_op jit(solution)/shard_map/ppermute | solution.py:71
  33.5 3.7 %collective-permute-start.40 = (f32[24,256]{1,0:T(8,128)S(1)}, f32[24,256]{1,0:T(8,128)S(1)}, u32[]{:S(2)}, u32[]{:S(2)}) collective-permute-start(f32[24,256]{1,0:T(8,128)S(1)} %get-tuple-element.352), channel_id=1, source_target_pairs={{0,16},{16,0},{1,17},{17,1},{2,18},{18,2},{3,19},{19,3},{4,20},{20... | collective-permute-start | bytes 73736 | tf_op jit(solution)/shard_map/ppermute | solution.py:565
  37.3 8.1 %collective-permute-start.41 = (f32[24,256]{1,0:T(8,128)S(1)}, f32[24,256]{1,0:T(8,128)S(1)}, u32[]{:S(2)}, u32[]{:S(2)}) collective-permute-start(f32[24,256]{1,0:T(8,128)S(1)} %add.458), channel_id=1, source_target_pairs={{0,1},{1,0},{2,3},{3,2},{4,5},{5,4},{6,7},{7,6},{8,9},{9,8},{10,11... | collective-permute-start | bytes 73736 | tf_op jit(solution)/shard_map/ppermute | solution.py:565
  42.0 5.3 %collective-permute-start.42 = (f32[24,256]{1,0:T(8,128)S(1)}, f32[24,256]{1,0:T(8,128)S(1)}, u32[]{:S(2)}, u32[]{:S(2)}) collective-permute-start(f32[24,256]{1,0:T(8,128)S(1)} %add.458), channel_id=1, source_target_pairs={{0,2},{1,3},{2,0},{3,1},{4,6},{5,7},{6,4},{7,5},{8,10},{9,11},{10,... | collective-permute-start | bytes 73736 | tf_op jit(solution)/shard_map/ppermute | solution.py:565
  45.3 5.0 %collective-permute-start.43 = (f32[24,256]{1,0:T(8,128)S(1)}, f32[24,256]{1,0:T(8,128)S(1)}, u32[]{:S(2)}, u32[]{:S(2)}) collective-permute-start(f32[24,256]{1,0:T(8,128)S(1)} %add.458), channel_id=1, source_target_pairs={{0,3},{1,2},{2,1},{3,0},{4,7},{5,6},{6,5},{7,4},{8,11},{9,10},{10,... | collective-permute-start | bytes 73736 | tf_op jit(solution)/shard_map/ppermute | solution.py:565
  50.4 4.8 %collective-permute-start.44 = (f32[24,256]{1,0:T(8,128)S(1)}, f32[24,256]{1,0:T(8,128)S(1)}, u32[]{:S(2)}, u32[]{:S(2)}) collective-permute-start(f32[24,256]{1,0:T(8,128)S(1)} %add_add_fusion.11), channel_id=1, source_target_pairs={{0,4},{4,0},{8,12},{12,8},{1,5},{5,1},{9,13},{13,9},{2,6},{6,2},{1... | collective-permute-start | bytes 73736 | tf_op jit(solution)/shard_map/ppermute | solution.py:565
  52.0 5.3 %collective-permute-start.45 = (f32[24,256]{1,0:T(8,128)S(1)}, f32[24,256]{1,0:T(8,128)S(1)}, u32[]{:S(2)}, u32[]{:S(2)}) collective-permute-start(f32[24,256]{1,0:T(8,128)S(1)} %add_add_fusion.11), channel_id=1, source_target_pairs={{0,8},{4,12},{8,0},{12,4},{1,9},{5,13},{9,1},{13,5},{2,10},{6,14},... | collective-permute-start | bytes 73736 | tf_op jit(solution)/shard_map/ppermute | solution.py:565
  53.7 5.0 %collective-permute-start.46 = (f32[24,256]{1,0:T(8,128)S(1)}, f32[24,256]{1,0:T(8,128)S(1)}, u32[]{:S(2)}, u32[]{:S(2)}) collective-permute-start(f32[24,256]{1,0:T(8,128)S(1)} %add_add_fusion.11), channel_id=1, source_target_pairs={{0,12},{4,8},{8,4},{12,0},{1,13},{5,9},{9,5},{13,1},{2,14},{6,10},... | collective-permute-start | bytes 73736 | tf_op jit(solution)/shard_map/ppermute | solution.py:565
  58.8 4.8 %collective-permute-start.47 = (f32[24,256]{1,0:T(8,128)S(1)}, f32[24,256]{1,0:T(8,128)S(1)}, u32[]{:S(2)}, u32[]{:S(2)}) collective-permute-start(f32[24,256]{1,0:T(8,128)S(1)} %add_add_fusion.10), channel_id=1, source_target_pairs={{0,32},{32,0},{64,96},{96,64},{1,33},{33,1},{65,97},{97,65},{2,34}... | collective-permute-start | bytes 73736 | tf_op jit(solution)/shard_map/ppermute | solution.py:565
  60.4 5.3 %collective-permute-start.48 = (f32[24,256]{1,0:T(8,128)S(1)}, f32[24,256]{1,0:T(8,128)S(1)}, u32[]{:S(2)}, u32[]{:S(2)}) collective-permute-start(f32[24,256]{1,0:T(8,128)S(1)} %add_add_fusion.10), channel_id=1, source_target_pairs={{0,64},{32,96},{64,0},{96,32},{1,65},{33,97},{65,1},{97,33},{2,66}... | collective-permute-start | bytes 73736 | tf_op jit(solution)/shard_map/ppermute | solution.py:565
  62.7 5.0 %collective-permute-start.49 = (f32[24,256]{1,0:T(8,128)S(1)}, f32[24,256]{1,0:T(8,128)S(1)}, u32[]{:S(2)}, u32[]{:S(2)}) collective-permute-start(f32[24,256]{1,0:T(8,128)S(1)} %add_add_fusion.10), channel_id=1, source_target_pairs={{0,96},{32,64},{64,32},{96,0},{1,97},{33,65},{65,33},{97,1},{2,98}... | collective-permute-start | bytes 73736 | tf_op jit(solution)/shard_map/ppermute | solution.py:565
  67.8 3.8 %copy-start.6 = (s32[32,128]{1,0:T(8,128)S(1)}, s32[32,128]{1,0:T(8,128)}, u32[]{:S(2)}) copy-start(s32[32,128]{1,0:T(8,128)} %eh_hbm.1) | copy-start | bytes 49156
  67.8 3.8 %copy-start.7 = (s32[32,128]{1,0:T(8,128)S(1)}, s32[32,128]{1,0:T(8,128)}, u32[]{:S(2)}) copy-start(s32[32,128]{1,0:T(8,128)} %ev_hbm.1) | copy-start | bytes 49156
  67.8 3.8 %copy-start.8 = (s32[32,128]{1,0:T(8,128)S(1)}, s32[32,128]{1,0:T(8,128)}, u32[]{:S(2)}) copy-start(s32[32,128]{1,0:T(8,128)} %pads_hbm.1) | copy-start | bytes 49156
  67.8 3.8 %copy-start.9 = (f32[256,8]{0,1:T(8,128)S(1)}, f32[256,8]{0,1:T(8,128)}, u32[]{:S(2)}) copy-start(f32[256,8]{0,1:T(8,128)} %param.16) | copy-start | bytes 24580

commit v3 on v2

--- a/solution.py
+++ b/solution.py
@@ -562,11 +562,13 @@
 def sum_everywhere(value):
     for axis in ("core", "z", "y", "x"):
         count = lax.axis_size(axis)
-        others = [lax.ppermute(value, axis, [(i, i ^ flip) for i in range(count)]) for flip in range(1, count)]
+        others = {
+            flip: lax.ppermute(value, axis, [(i, i ^ flip) for i in range(count)]) for flip in range(count - 1, 0, -1)
+        }
         if count == 4:
-            value = (value + others[0]) + (others[1] + others[2])
+            value = (value + others[3]) + (others[2] + others[1])
         else:
-            value = value + others[0]
+            value = value + others[1]
     return value
 
 

time: 72.2 us -> 69 us (0.956)
  starting transfers between devices: 24 us -> 22.3 us
  waiting for transfers between devices: 13.7 us -> 12.3 us
    ppermute x10, starting transfers between devices: 20.5 us -> 18.8 us  [sum_everywhere(): lax.ppermute(value, axis, [(i, i ^ flip) for i in range(count)])]
    ppermute x10, waiting for transfers between devices: 13.7 us -> 12.3 us  [sum_everywhere(): lax.ppermute(value, axis, [(i, i ^ flip) for i in range(count)])]
  transfers between devices with their start and end apart: 14 -> 14, of which waited for: 7 -> 8; matrix products, arithmetic and copies ran while one was open for 0% -> 0% of each run, Pallas kernels for 26% -> 27%
where the time goes in v3:
time: 69 us; the launch traced here: 68.8 us
  Pallas kernels  32.4 us (47%)
  starting transfers between devices  22.3 us (32%)
  waiting for transfers between devices  12.3 us (18%)
  between operations  1.55 us (2%)
    ppermute x10, starting transfers between devices, sum_everywhere(): lax.ppermute(value, axis, [(i, i ^ flip) for i in range(count)])  18.8 us
    pallas_call x1, Pallas kernels, basis(): pl.pallas_call(lambda *refs: inner_kernel(grid, *refs), in_specs=[ON_CHIP...  14.4 us
    ppermute x10, waiting for transfers between devices, sum_everywhere(): lax.ppermute(value, axis, [(i, i ^ flip) for i in range(count)])  12.3 us
    pallas_call x1, Pallas kernels, basis(): pl.pallas_call(lambda *refs: outer_kernel(grid, *refs), in_specs=[ON_CHIP...  6.28 us
    pallas_call x1, Pallas kernels, basis(): pl.pallas_call(lambda *refs: own_kernel(grid, *refs), in_specs=[ON_CHIP]...  4.35 us
    pallas_call x1, Pallas kernels, prepare(): pl.pallas_call(prepare_kernel, in_specs=[IN_HBM] * 5, out_specs=[ON_CHIP]...  4.14 us
    pallas_call x1, Pallas kernels, combine(): pl.pallas_call(combine_kernel, in_specs=[ON_CHIP] * 5, out_specs=[IN_HBM,...  3.17 us
    ppermute x2, starting transfers between devices, swaps(): lax.ppermute(first, axes, [(i, i ^ 1) for i in range(count)])  2.17 us
  transfers between devices with their start and end apart: 14, of which 8 were waited for; matrix products, arithmetic and copies ran while one was open for 0% of the time, Pallas kernels for 27%

profile of v3, /device:TPU:0, one launch (start us, length us, event | category | flops | bytes accessed | tf_op | source)
XLA Modules:
  0.0 68.8 jit_solution(1501004228097244290)
XLA Ops:
  0.6 4.1 %shard_map.78 = (f32[32,128,256]{2,1,0:T(8,128)S(1)}, f32[128,128]{1,0:T(8,128)S(1)}, f32[17,8,256]{2,1,0:T(8,128)S(1)}, f32[17,8,256]{2,1,0:T(8,128)S(1)}) custom-call(s32[256,32,128]{2,1,0:T(8,128)} %loads_hbm.1, f32[8,256]{1,0:T(8,128)} %bitcast.36, s32[32,128]{1,0:T(8,128)} %eh_hbm.1, s32[32,128]{1,0:T(8,128)} %ev_hbm.1, s32[32,128]{1,0:T(8,128)} %pads_hbm.1), custom_call_target="tpu_custom_call" | custom-call | flops 20000000 | bytes 12582912 | tf_op jit(solution)/shard_map/pallas_call | solution.py:131
  4.8 2.1 %collective-permute-start.36 = (f32[17,8,256]{2,1,0:T(8,128)S(1)}, f32[17,8,256]{2,1,0:T(8,128)S(1)}, u32[]{:S(2)}, u32[]{:S(2)}) collective-permute-start(f32[17,8,256]{2,1,0:T(8,128)S(1)} %get-tuple-element.334), channel_id=1, source_target_pairs={{0,1},{1,0},{2,3},{3,2},{4,5},{5,4},{6,7},{7,6},{8,9},{9,8},{10,11... | collective-permute-start | bytes 417800 | tf_op jit(solution)/shard_map/ppermute | solution.py:70
  6.9 0.7 collective-permute-start.37
  7.5 4.4 %shard_map.79 = (f32[40,160,128]{2,1,0:T(8,128)S(1)}, f32[40,160,128]{2,1,0:T(8,128)S(1)}, f32[40,160,128]{2,1,0:T(8,128)S(1)}, f32[40,160,128]{2,1,0:T(8,128)S(1)}, f32[2,40,160,128]{3,2,1,0:T(8,128)S(1)}) custom-call(f32[32,128,256]{2,1,0:T(8,128)S(1)} %get-tuple-element.332.refs_0_.rhs_ref, f32[128,128]{1,0:T(8,128)S(1)} %get-tuple-element.333.refs_1_.turned_ref), custom_call_target="tpu_custom_call" | custom-call | bytes 24000000 | tf_op jit(solution)/shard_map/pallas_call | solution.py:417
  11.9 0.0 collective-permute-done.36.side_a.refs_2_
  11.9 0.0 collective-permute-done.37.side_b.refs_3_
  11.9 0.1 shard_map.80
  12.0 0.1 collective-permute-start.38
  12.1 0.7 %collective-permute-start.39 = (f32[77,8,256]{2,1,0:T(8,128)S(1)}, f32[77,8,256]{2,1,0:T(8,128)S(1)}, u32[]{:S(2)}, u32[]{:S(2)}) collective-permute-start(f32[77,8,256]{2,1,0:T(8,128)S(1)} %get-tuple-element.338), channel_id=1, source_target_pairs={{16,32},{48,64},{80,96},{32,16},{64,48},{96,80},{17,33},{49,65},{8... | collective-permute-start | bytes 1892360 | tf_op jit(solution)/shard_map/ppermute | solution.py:71
  12.8 14.4 %shard_map.81 = (f32[40,160,128]{2,1,0:T(8,128)S(1)}, f32[40,160,128]{2,1,0:T(8,128)S(1)}, f32[40,160,128]{2,1,0:T(8,128)S(1)}, f32[40,160,128]{2,1,0:T(8,128)S(...) custom-call(f32[32,128,256]{2,1,0:T(8,128)S(1)} %get-tuple-element.3, ...), custom_call_target="tpu_custom_call", output_to_operand_aliasing={{0}: (4, {}), {1}: (5, {}), {2}: (6, {}), {3}: (7, {}), {4}... | custom-call | bytes 42000000 | tf_op jit(solution)/shard_map/pallas_call | solution.py:427
  27.2 0.0 collective-permute-done.38.refs_4_
  27.2 0.0 collective-permute-done.39.refs_5_
  27.2 6.3 %shard_map.82 = (f32[40,160,128]{2,1,0:T(8,128)S(1)}, f32[40,160,128]{2,1,0:T(8,128)S(1)}, f32[40,160,128]{2,1,0:T(8,128)S(1)}, f32[40,160,128]{2,1,0:T(8,128)S(...) custom-call(f32[32,128,256]{2,1,0:T(8,128)S(1)} %get-tuple-element.3, ...), custom_call_target="tpu_custom_call", output_to_operand_aliasing={{0}: (7, {}), {1}: (8, {}), {2}: (9, {}), {3}: (10, {}), {4... | custom-call | bytes 21000000 | tf_op jit(solution)/shard_map/pallas_call | solution.py:438
  33.5 2.9 %collective-permute-start.40 = (f32[24,256]{1,0:T(8,128)S(1)}, f32[24,256]{1,0:T(8,128)S(1)}, u32[]{:S(2)}, u32[]{:S(2)}) collective-permute-start(f32[24,256]{1,0:T(8,128)S(1)} %get-tuple-element.352), channel_id=1, source_target_pairs={{0,16},{16,0},{1,17},{17,1},{2,18},{18,2},{3,19},{19,3},{4,20},{20... | collective-permute-start | bytes 73736 | tf_op jit(solution)/shard_map/ppermute | solution.py:566
  36.4 0.8 %collective-permute-done.40 = f32[24,256]{1,0:T(8,128)S(1)} collective-permute-done((f32[24,256]{1,0:T(8,128)S(1)}, f32[24,256]{1,0:T(8,128)S(1)}, u32[]{:S(2)}, u32[]{:S(2)}) %collective-permute-start.40) | collective-permute-done | bytes 24608 | tf_op jit(solution)/shard_map/ppermute | solution.py:566
  37.3 6.6 %collective-permute-start.41 = (f32[24,256]{1,0:T(8,128)S(1)}, f32[24,256]{1,0:T(8,128)S(1)}, u32[]{:S(2)}, u32[]{:S(2)}) collective-permute-start(f32[24,256]{1,0:T(8,128)S(1)} %add.458), channel_id=1, source_target_pairs={{0,3},{1,2},{2,1},{3,0},{4,7},{5,6},{6,5},{7,4},{8,11},{9,10},{10,... | collective-permute-start | bytes 73736 | tf_op jit(solution)/shard_map/ppermute | solution.py:566
  43.9 0.3 collective-permute-start.42
  44.1 0.7 collective-permute-start.43
  44.8 0.9 %collective-permute-done.41 = f32[24,256]{1,0:T(8,128)S(1)} collective-permute-done((f32[24,256]{1,0:T(8,128)S(1)}, f32[24,256]{1,0:T(8,128)S(1)}, u32[]{:S(2)}, u32[]{:S(2)}) %collective-permute-start.41) | collective-permute-done | bytes 24608 | tf_op jit(solution)/shard_map/ppermute | solution.py:566
  45.7 3.5 %collective-permute-done.42 = f32[24,256]{1,0:T(8,128)S(1)} collective-permute-done((f32[24,256]{1,0:T(8,128)S(1)}, f32[24,256]{1,0:T(8,128)S(1)}, u32[]{:S(2)}, u32[]{:S(2)}) %collective-permute-start.42) | collective-permute-done | bytes 24608 | tf_op jit(solution)/shard_map/ppermute | solution.py:566
  49.2 0.0 collective-permute-done.43
  49.2 1.8 %collective-permute-start.44 = (f32[24,256]{1,0:T(8,128)S(1)}, f32[24,256]{1,0:T(8,128)S(1)}, u32[]{:S(2)}, u32[]{:S(2)}) collective-permute-start(f32[24,256]{1,0:T(8,128)S(1)} %add_add_fusion.11), channel_id=1, source_target_pairs={{0,12},{4,8},{8,4},{12,0},{1,13},{5,9},{9,5},{13,1},{2,14},{6,10},... | collective-permute-start | bytes 73736 | tf_op jit(solution)/shard_map/ppermute | solution.py:566
  51.0 1.9 %collective-permute-start.45 = (f32[24,256]{1,0:T(8,128)S(1)}, f32[24,256]{1,0:T(8,128)S(1)}, u32[]{:S(2)}, u32[]{:S(2)}) collective-permute-start(f32[24,256]{1,0:T(8,128)S(1)} %add_add_fusion.11), channel_id=1, source_target_pairs={{0,8},{4,12},{8,0},{12,4},{1,9},{5,13},{9,1},{13,5},{2,10},{6,14},... | collective-permute-start | bytes 73736 | tf_op jit(solution)/shard_map/ppermute | solution.py:566
  52.9 0.5 collective-permute-start.46
  53.4 0.9 %collective-permute-done.44 = f32[24,256]{1,0:T(8,128)S(1)} collective-permute-done((f32[24,256]{1,0:T(8,128)S(1)}, f32[24,256]{1,0:T(8,128)S(1)}, u32[]{:S(2)}, u32[]{:S(2)}) %collective-permute-start.44) | collective-permute-done | bytes 24608 | tf_op jit(solution)/shard_map/ppermute | solution.py:566
  54.3 2.1 %collective-permute-done.45 = f32[24,256]{1,0:T(8,128)S(1)} collective-permute-done((f32[24,256]{1,0:T(8,128)S(1)}, f32[24,256]{1,0:T(8,128)S(1)}, u32[]{:S(2)}, u32[]{:S(2)}) %collective-permute-start.45) | collective-permute-done | bytes 24608 | tf_op jit(solution)/shard_map/ppermute | solution.py:566
  56.4 0.4 collective-permute-done.46
  56.8 2.5 %collective-permute-start.47 = (f32[24,256]{1,0:T(8,128)S(1)}, f32[24,256]{1,0:T(8,128)S(1)}, u32[]{:S(2)}, u32[]{:S(2)}) collective-permute-start(f32[24,256]{1,0:T(8,128)S(1)} %add_add_fusion.10), channel_id=1, source_target_pairs={{0,96},{32,64},{64,32},{96,0},{1,97},{33,65},{65,33},{97,1},{2,98}... | collective-permute-start | bytes 73736 | tf_op jit(solution)/shard_map/ppermute | solution.py:566
  59.3 1.1 %collective-permute-start.48 = (f32[24,256]{1,0:T(8,128)S(1)}, f32[24,256]{1,0:T(8,128)S(1)}, u32[]{:S(2)}, u32[]{:S(2)}) collective-permute-start(f32[24,256]{1,0:T(8,128)S(1)} %add_add_fusion.10), channel_id=1, source_target_pairs={{0,64},{32,96},{64,0},{96,32},{1,65},{33,97},{65,1},{97,33},{2,66}... | collective-permute-start | bytes 73736 | tf_op jit(solution)/shard_map/ppermute | solution.py:566
  60.4 0.5 collective-permute-start.49
  60.9 0.9 %collective-permute-done.47 = f32[24,256]{1,0:T(8,128)S(1)} collective-permute-done((f32[24,256]{1,0:T(8,128)S(1)}, f32[24,256]{1,0:T(8,128)S(1)}, u32[]{:S(2)}, u32[]{:S(2)}) %collective-permute-start.47) | collective-permute-done | bytes 24608 | tf_op jit(solution)/shard_map/ppermute | solution.py:566
  61.9 2.7 %collective-permute-done.48 = f32[24,256]{1,0:T(8,128)S(1)} collective-permute-done((f32[24,256]{1,0:T(8,128)S(1)}, f32[24,256]{1,0:T(8,128)S(1)}, u32[]{:S(2)}, u32[]{:S(2)}) %collective-permute-start.48) | collective-permute-done | bytes 24608 | tf_op jit(solution)/shard_map/ppermute | solution.py:566
  64.6 0.0 collective-permute-done.49
  64.6 0.0 copy-start.6
  64.6 0.0 copy-start.7
  64.6 0.0 copy-start.8
  64.6 0.0 copy-start.9
  64.7 3.2 %shard_map.83 = (f32[256,32,128]{2,1,0:T(8,128)}, f32[5,256]{1,0:T(8,128)}, s32[1]{0:T(128)}) custom-call(f32[24,256]{1,0:T(8,128)S(1)} %add_add_fusion.9.sums_ref, f32[2,40,160,128]{3,2,1,0:T(8,128)S(1)} %get-tuple-element.353.v0, f32[2,40,160,128]{3,2,1,0:T(8,128)S(1)} %get-tuple-element.354.v1, f32[2,40,160,128]{3,2,1,0:T(8,128)S(1)} %get-tuple-element.355.v2, ...), custom_call_target="tpu_custom_call" | custom-call | tf_op jit(solution)/shard_map/pallas_call | solution.py:543
  68.4 0.0 copy-done.6
  68.4 0.0 copy-done.7
  68.4 0.0 copy-done.8
  68.4 0.0 copy-done.9
  68.4 0.2 conditional.1
  (4 shorter events, 0.0 us)
Async XLA Ops:
  4.8 7.1 %collective-permute-start.36 = (f32[17,8,256]{2,1,0:T(8,128)S(1)}, f32[17,8,256]{2,1,0:T(8,128)S(1)}, u32[]{:S(2)}, u32[]{:S(2)}) collective-permute-start(f32[17,8,256]{2,1,0:T(8,128)S(1)} %get-tuple-element.334), channel_id=1, source_target_pairs={{0,1},{1,0},{2,3},{3,2},{4,5},{5,4},{6,7},{7,6},{8,9},{9,8},{10,11... | collective-permute-start | bytes 417800 | tf_op jit(solution)/shard_map/ppermute | solution.py:70
  6.9 5.0 %collective-permute-start.37 = (f32[17,8,256]{2,1,0:T(8,128)S(1)}, f32[17,8,256]{2,1,0:T(8,128)S(1)}, u32[]{:S(2)}, u32[]{:S(2)}) collective-permute-start(f32[17,8,256]{2,1,0:T(8,128)S(1)} %get-tuple-element.335), channel_id=1, source_target_pairs={{1,2},{3,4},{5,6},{7,8},{9,10},{11,12},{13,14},{2,1},{4,3},{6,5},{... | collective-permute-start | bytes 417800 | tf_op jit(solution)/shard_map/ppermute | solution.py:71
  12.0 15.2 %collective-permute-start.38 = (f32[77,8,256]{2,1,0:T(8,128)S(1)}, f32[77,8,256]{2,1,0:T(8,128)S(1)}, u32[]{:S(2)}, u32[]{:S(2)}) collective-permute-start(f32[77,8,256]{2,1,0:T(8,128)S(1)} %get-tuple-element.337), channel_id=1, source_target_pairs={{0,16},{16,0},{32,48},{48,32},{64,80},{80,64},{96,112},{112,96},{1... | collective-permute-start | bytes 1892360 | tf_op jit(solution)/shard_map/ppermute | solution.py:70
  12.1 15.1 %collective-permute-start.39 = (f32[77,8,256]{2,1,0:T(8,128)S(1)}, f32[77,8,256]{2,1,0:T(8,128)S(1)}, u32[]{:S(2)}, u32[]{:S(2)}) collective-permute-start(f32[77,8,256]{2,1,0:T(8,128)S(1)} %get-tuple-element.338), channel_id=1, source_target_pairs={{16,32},{48,64},{80,96},{32,16},{64,48},{96,80},{17,33},{49,65},{8... | collective-permute-start | bytes 1892360 | tf_op jit(solution)/shard_map/ppermute | solution.py:71
  33.5 3.7 %collective-permute-start.40 = (f32[24,256]{1,0:T(8,128)S(1)}, f32[24,256]{1,0:T(8,128)S(1)}, u32[]{:S(2)}, u32[]{:S(2)}) collective-permute-start(f32[24,256]{1,0:T(8,128)S(1)} %get-tuple-element.352), channel_id=1, source_target_pairs={{0,16},{16,0},{1,17},{17,1},{2,18},{18,2},{3,19},{19,3},{4,20},{20... | collective-permute-start | bytes 73736 | tf_op jit(solution)/shard_map/ppermute | solution.py:566
  37.3 8.4 %collective-permute-start.41 = (f32[24,256]{1,0:T(8,128)S(1)}, f32[24,256]{1,0:T(8,128)S(1)}, u32[]{:S(2)}, u32[]{:S(2)}) collective-permute-start(f32[24,256]{1,0:T(8,128)S(1)} %add.458), channel_id=1, source_target_pairs={{0,3},{1,2},{2,1},{3,0},{4,7},{5,6},{6,5},{7,4},{8,11},{9,10},{10,... | collective-permute-start | bytes 73736 | tf_op jit(solution)/shard_map/ppermute | solution.py:566
  43.9 5.3 %collective-permute-start.42 = (f32[24,256]{1,0:T(8,128)S(1)}, f32[24,256]{1,0:T(8,128)S(1)}, u32[]{:S(2)}, u32[]{:S(2)}) collective-permute-start(f32[24,256]{1,0:T(8,128)S(1)} %add.458), channel_id=1, source_target_pairs={{0,2},{1,3},{2,0},{3,1},{4,6},{5,7},{6,4},{7,5},{8,10},{9,11},{10,... | collective-permute-start | bytes 73736 | tf_op jit(solution)/shard_map/ppermute | solution.py:566
  44.1 5.1 %collective-permute-start.43 = (f32[24,256]{1,0:T(8,128)S(1)}, f32[24,256]{1,0:T(8,128)S(1)}, u32[]{:S(2)}, u32[]{:S(2)}) collective-permute-start(f32[24,256]{1,0:T(8,128)S(1)} %add.458), channel_id=1, source_target_pairs={{0,1},{1,0},{2,3},{3,2},{4,5},{5,4},{6,7},{7,6},{8,9},{9,8},{10,11... | collective-permute-start | bytes 73736 | tf_op jit(solution)/shard_map/ppermute | solution.py:566
  49.2 5.1 %collective-permute-start.44 = (f32[24,256]{1,0:T(8,128)S(1)}, f32[24,256]{1,0:T(8,128)S(1)}, u32[]{:S(2)}, u32[]{:S(2)}) collective-permute-start(f32[24,256]{1,0:T(8,128)S(1)} %add_add_fusion.11), channel_id=1, source_target_pairs={{0,12},{4,8},{8,4},{12,0},{1,13},{5,9},{9,5},{13,1},{2,14},{6,10},... | collective-permute-start | bytes 73736 | tf_op jit(solution)/shard_map/ppermute | solution.py:566
  51.0 5.3 %collective-permute-start.45 = (f32[24,256]{1,0:T(8,128)S(1)}, f32[24,256]{1,0:T(8,128)S(1)}, u32[]{:S(2)}, u32[]{:S(2)}) collective-permute-start(f32[24,256]{1,0:T(8,128)S(1)} %add_add_fusion.11), channel_id=1, source_target_pairs={{0,8},{4,12},{8,0},{12,4},{1,9},{5,13},{9,1},{13,5},{2,10},{6,14},... | collective-permute-start | bytes 73736 | tf_op jit(solution)/shard_map/ppermute | solution.py:566
  52.9 3.8 %collective-permute-start.46 = (f32[24,256]{1,0:T(8,128)S(1)}, f32[24,256]{1,0:T(8,128)S(1)}, u32[]{:S(2)}, u32[]{:S(2)}) collective-permute-start(f32[24,256]{1,0:T(8,128)S(1)} %add_add_fusion.11), channel_id=1, source_target_pairs={{0,4},{4,0},{8,12},{12,8},{1,5},{5,1},{9,13},{13,9},{2,6},{6,2},{1... | collective-permute-start | bytes 73736 | tf_op jit(solution)/shard_map/ppermute | solution.py:566
  56.8 5.1 %collective-permute-start.47 = (f32[24,256]{1,0:T(8,128)S(1)}, f32[24,256]{1,0:T(8,128)S(1)}, u32[]{:S(2)}, u32[]{:S(2)}) collective-permute-start(f32[24,256]{1,0:T(8,128)S(1)} %add_add_fusion.10), channel_id=1, source_target_pairs={{0,96},{32,64},{64,32},{96,0},{1,97},{33,65},{65,33},{97,1},{2,98}... | collective-permute-start | bytes 73736 | tf_op jit(solution)/shard_map/ppermute | solution.py:566
  59.3 5.3 %collective-permute-start.48 = (f32[24,256]{1,0:T(8,128)S(1)}, f32[24,256]{1,0:T(8,128)S(1)}, u32[]{:S(2)}, u32[]{:S(2)}) collective-permute-start(f32[24,256]{1,0:T(8,128)S(1)} %add_add_fusion.10), channel_id=1, source_target_pairs={{0,64},{32,96},{64,0},{96,32},{1,65},{33,97},{65,1},{97,33},{2,66}... | collective-permute-start | bytes 73736 | tf_op jit(solution)/shard_map/ppermute | solution.py:566
  60.4 4.2 %collective-permute-start.49 = (f32[24,256]{1,0:T(8,128)S(1)}, f32[24,256]{1,0:T(8,128)S(1)}, u32[]{:S(2)}, u32[]{:S(2)}) collective-permute-start(f32[24,256]{1,0:T(8,128)S(1)} %add_add_fusion.10), channel_id=1, source_target_pairs={{0,32},{32,0},{64,96},{96,64},{1,33},{33,1},{65,97},{97,65},{2,34}... | collective-permute-start | bytes 73736 | tf_op jit(solution)/shard_map/ppermute | solution.py:566
  64.6 3.8 %copy-start.6 = (s32[32,128]{1,0:T(8,128)S(1)}, s32[32,128]{1,0:T(8,128)}, u32[]{:S(2)}) copy-start(s32[32,128]{1,0:T(8,128)} %eh_hbm.1) | copy-start | bytes 49156
  64.6 3.8 %copy-start.7 = (s32[32,128]{1,0:T(8,128)S(1)}, s32[32,128]{1,0:T(8,128)}, u32[]{:S(2)}) copy-start(s32[32,128]{1,0:T(8,128)} %ev_hbm.1) | copy-start | bytes 49156
  64.6 3.8 %copy-start.8 = (s32[32,128]{1,0:T(8,128)S(1)}, s32[32,128]{1,0:T(8,128)}, u32[]{:S(2)}) copy-start(s32[32,128]{1,0:T(8,128)} %pads_hbm.1) | copy-start | bytes 49156
  64.6 3.8 %copy-start.9 = (f32[256,8]{0,1:T(8,128)S(1)}, f32[256,8]{0,1:T(8,128)}, u32[]{:S(2)}) copy-start(f32[256,8]{0,1:T(8,128)} %param.16) | copy-start | bytes 24580

commit v4 on v3

--- a/solution.py
+++ b/solution.py
@@ -394,7 +394,7 @@
                     v0[half, row, tile_at(tile), :] = value * di_ref[row, tile_at(tile), :]
     for level in range(1, ITERS):
         runs = (range(level - HALO, level + 1), range(rows - level, rows + HALO - level))
-        step(fields[level - 1], fields[level], coef, runs, reach, 3)
+        step(fields[level - 1], fields[level], coef, runs, reach, 6)
     for half in range(scen // LANES):
         sums = [inner_ref[half, number] for number in range(COUNT)]
         sums = gram(fields, coef, half, (*range(ITERS + 1), *range(rows - ITERS, rows)), own, sums)

time: 69 us -> 69.2 us (level)
  no operation moved by 1% of the time
where the time goes in v4:
time: 69.2 us; the launch traced here: 69 us
  Pallas kernels  32.3 us (47%)
  starting transfers between devices  22.6 us (33%)
  waiting for transfers between devices  12.3 us (18%)
  between operations  1.55 us (2%)
    ppermute x10, starting transfers between devices, sum_everywhere(): lax.ppermute(value, axis, [(i, i ^ flip) for i in range(count)])  19.1 us
    pallas_call x1, Pallas kernels, basis(): pl.pallas_call(lambda *refs: inner_kernel(grid, *refs), in_specs=[ON_CHIP...  14.4 us
    ppermute x10, waiting for transfers between devices, sum_everywhere(): lax.ppermute(value, axis, [(i, i ^ flip) for i in range(count)])  12.3 us
    pallas_call x1, Pallas kernels, basis(): pl.pallas_call(lambda *refs: outer_kernel(grid, *refs), in_specs=[ON_CHIP...  6.19 us
    pallas_call x1, Pallas kernels, basis(): pl.pallas_call(lambda *refs: own_kernel(grid, *refs), in_specs=[ON_CHIP]...  4.35 us
    pallas_call x1, Pallas kernels, prepare(): pl.pallas_call(prepare_kernel, in_specs=[IN_HBM] * 5, out_specs=[ON_CHIP]...  4.14 us
    pallas_call x1, Pallas kernels, combine(): pl.pallas_call(combine_kernel, in_specs=[ON_CHIP] * 5, out_specs=[IN_HBM,...  3.17 us
    ppermute x2, starting transfers between devices, swaps(): lax.ppermute(first, axes, [(i, i ^ 1) for i in range(count)])  2.17 us
  transfers between devices with their start and end apart: 14, of which 8 were waited for; matrix products, arithmetic and copies ran while one was open for 0% of the time, Pallas kernels for 27%

profile of v4, /device:TPU:0, one launch (start us, length us, event | category | flops | bytes accessed | tf_op | source)
XLA Modules:
  0.0 69.0 jit_solution(1822038921658809266)
XLA Ops:
  0.6 4.1 %shard_map.78 = (f32[32,128,256]{2,1,0:T(8,128)S(1)}, f32[128,128]{1,0:T(8,128)S(1)}, f32[17,8,256]{2,1,0:T(8,128)S(1)}, f32[17,8,256]{2,1,0:T(8,128)S(1)}) custom-call(s32[256,32,128]{2,1,0:T(8,128)} %loads_hbm.1, f32[8,256]{1,0:T(8,128)} %bitcast.36, s32[32,128]{1,0:T(8,128)} %eh_hbm.1, s32[32,128]{1,0:T(8,128)} %ev_hbm.1, s32[32,128]{1,0:T(8,128)} %pads_hbm.1), custom_call_target="tpu_custom_call" | custom-call | flops 20000000 | bytes 12582912 | tf_op jit(solution)/shard_map/pallas_call | solution.py:131
  4.8 2.1 %collective-permute-start.36 = (f32[17,8,256]{2,1,0:T(8,128)S(1)}, f32[17,8,256]{2,1,0:T(8,128)S(1)}, u32[]{:S(2)}, u32[]{:S(2)}) collective-permute-start(f32[17,8,256]{2,1,0:T(8,128)S(1)} %get-tuple-element.334), channel_id=1, source_target_pairs={{0,1},{1,0},{2,3},{3,2},{4,5},{5,4},{6,7},{7,6},{8,9},{9,8},{10,11... | collective-permute-start | bytes 417800 | tf_op jit(solution)/shard_map/ppermute | solution.py:70
  6.9 0.7 collective-permute-start.37
  7.5 4.4 %shard_map.79 = (f32[40,160,128]{2,1,0:T(8,128)S(1)}, f32[40,160,128]{2,1,0:T(8,128)S(1)}, f32[40,160,128]{2,1,0:T(8,128)S(1)}, f32[40,160,128]{2,1,0:T(8,128)S(1)}, f32[2,40,160,128]{3,2,1,0:T(8,128)S(1)}) custom-call(f32[32,128,256]{2,1,0:T(8,128)S(1)} %get-tuple-element.332.refs_0_.rhs_ref, f32[128,128]{1,0:T(8,128)S(1)} %get-tuple-element.333.refs_1_.turned_ref), custom_call_target="tpu_custom_call" | custom-call | bytes 24000000 | tf_op jit(solution)/shard_map/pallas_call | solution.py:417
  11.9 0.0 collective-permute-done.36.side_a.refs_2_
  11.9 0.0 collective-permute-done.37.side_b.refs_3_
  11.9 0.1 shard_map.80
  12.0 0.1 collective-permute-start.38
  12.1 0.7 %collective-permute-start.39 = (f32[77,8,256]{2,1,0:T(8,128)S(1)}, f32[77,8,256]{2,1,0:T(8,128)S(1)}, u32[]{:S(2)}, u32[]{:S(2)}) collective-permute-start(f32[77,8,256]{2,1,0:T(8,128)S(1)} %get-tuple-element.338), channel_id=1, source_target_pairs={{16,32},{48,64},{80,96},{32,16},{64,48},{96,80},{17,33},{49,65},{8... | collective-permute-start | bytes 1892360 | tf_op jit(solution)/shard_map/ppermute | solution.py:71
  12.8 14.4 %shard_map.81 = (f32[40,160,128]{2,1,0:T(8,128)S(1)}, f32[40,160,128]{2,1,0:T(8,128)S(1)}, f32[40,160,128]{2,1,0:T(8,128)S(1)}, f32[40,160,128]{2,1,0:T(8,128)S(...) custom-call(f32[32,128,256]{2,1,0:T(8,128)S(1)} %get-tuple-element.3, ...), custom_call_target="tpu_custom_call", output_to_operand_aliasing={{0}: (4, {}), {1}: (5, {}), {2}: (6, {}), {3}: (7, {}), {4}... | custom-call | bytes 42000000 | tf_op jit(solution)/shard_map/pallas_call | solution.py:427
  27.2 0.0 collective-permute-done.38.refs_4_
  27.2 0.0 collective-permute-done.39.refs_5_
  27.2 6.2 %shard_map.82 = (f32[40,160,128]{2,1,0:T(8,128)S(1)}, f32[40,160,128]{2,1,0:T(8,128)S(1)}, f32[40,160,128]{2,1,0:T(8,128)S(1)}, f32[40,160,128]{2,1,0:T(8,128)S(...) custom-call(f32[32,128,256]{2,1,0:T(8,128)S(1)} %get-tuple-element.3, ...), custom_call_target="tpu_custom_call", output_to_operand_aliasing={{0}: (7, {}), {1}: (8, {}), {2}: (9, {}), {3}: (10, {}), {4... | custom-call | bytes 21000000 | tf_op jit(solution)/shard_map/pallas_call | solution.py:438
  33.4 2.9 %collective-permute-start.40 = (f32[24,256]{1,0:T(8,128)S(1)}, f32[24,256]{1,0:T(8,128)S(1)}, u32[]{:S(2)}, u32[]{:S(2)}) collective-permute-start(f32[24,256]{1,0:T(8,128)S(1)} %get-tuple-element.352), channel_id=1, source_target_pairs={{0,16},{16,0},{1,17},{17,1},{2,18},{18,2},{3,19},{19,3},{4,20},{20... | collective-permute-start | bytes 73736 | tf_op jit(solution)/shard_map/ppermute | solution.py:566
  36.3 0.8 %collective-permute-done.40 = f32[24,256]{1,0:T(8,128)S(1)} collective-permute-done((f32[24,256]{1,0:T(8,128)S(1)}, f32[24,256]{1,0:T(8,128)S(1)}, u32[]{:S(2)}, u32[]{:S(2)}) %collective-permute-start.40) | collective-permute-done | bytes 24608 | tf_op jit(solution)/shard_map/ppermute | solution.py:566
  37.2 6.6 %collective-permute-start.41 = (f32[24,256]{1,0:T(8,128)S(1)}, f32[24,256]{1,0:T(8,128)S(1)}, u32[]{:S(2)}, u32[]{:S(2)}) collective-permute-start(f32[24,256]{1,0:T(8,128)S(1)} %add.458), channel_id=1, source_target_pairs={{0,3},{1,2},{2,1},{3,0},{4,7},{5,6},{6,5},{7,4},{8,11},{9,10},{10,... | collective-permute-start | bytes 73736 | tf_op jit(solution)/shard_map/ppermute | solution.py:566
  43.8 0.3 collective-permute-start.42
  44.0 0.7 collective-permute-start.43
  44.7 0.9 %collective-permute-done.41 = f32[24,256]{1,0:T(8,128)S(1)} collective-permute-done((f32[24,256]{1,0:T(8,128)S(1)}, f32[24,256]{1,0:T(8,128)S(1)}, u32[]{:S(2)}, u32[]{:S(2)}) %collective-permute-start.41) | collective-permute-done | bytes 24608 | tf_op jit(solution)/shard_map/ppermute | solution.py:566
  45.6 3.5 %collective-permute-done.42 = f32[24,256]{1,0:T(8,128)S(1)} collective-permute-done((f32[24,256]{1,0:T(8,128)S(1)}, f32[24,256]{1,0:T(8,128)S(1)}, u32[]{:S(2)}, u32[]{:S(2)}) %collective-permute-start.42) | collective-permute-done | bytes 24608 | tf_op jit(solution)/shard_map/ppermute | solution.py:566
  49.1 0.0 collective-permute-done.43
  49.1 1.8 %collective-permute-start.44 = (f32[24,256]{1,0:T(8,128)S(1)}, f32[24,256]{1,0:T(8,128)S(1)}, u32[]{:S(2)}, u32[]{:S(2)}) collective-permute-start(f32[24,256]{1,0:T(8,128)S(1)} %add_add_fusion.11), channel_id=1, source_target_pairs={{0,12},{4,8},{8,4},{12,0},{1,13},{5,9},{9,5},{13,1},{2,14},{6,10},... | collective-permute-start | bytes 73736 | tf_op jit(solution)/shard_map/ppermute | solution.py:566
  51.0 1.9 %collective-permute-start.45 = (f32[24,256]{1,0:T(8,128)S(1)}, f32[24,256]{1,0:T(8,128)S(1)}, u32[]{:S(2)}, u32[]{:S(2)}) collective-permute-start(f32[24,256]{1,0:T(8,128)S(1)} %add_add_fusion.11), channel_id=1, source_target_pairs={{0,8},{4,12},{8,0},{12,4},{1,9},{5,13},{9,1},{13,5},{2,10},{6,14},... | collective-permute-start | bytes 73736 | tf_op jit(solution)/shard_map/ppermute | solution.py:566
  52.8 0.5 collective-permute-start.46
  53.3 0.9 %collective-permute-done.44 = f32[24,256]{1,0:T(8,128)S(1)} collective-permute-done((f32[24,256]{1,0:T(8,128)S(1)}, f32[24,256]{1,0:T(8,128)S(1)}, u32[]{:S(2)}, u32[]{:S(2)}) %collective-permute-start.44) | collective-permute-done | bytes 24608 | tf_op jit(solution)/shard_map/ppermute | solution.py:566
  54.2 2.1 %collective-permute-done.45 = f32[24,256]{1,0:T(8,128)S(1)} collective-permute-done((f32[24,256]{1,0:T(8,128)S(1)}, f32[24,256]{1,0:T(8,128)S(1)}, u32[]{:S(2)}, u32[]{:S(2)}) %collective-permute-start.45) | collective-permute-done | bytes 24608 | tf_op jit(solution)/shard_map/ppermute | solution.py:566
  56.3 0.4 collective-permute-done.46
  56.7 2.8 %collective-permute-start.47 = (f32[24,256]{1,0:T(8,128)S(1)}, f32[24,256]{1,0:T(8,128)S(1)}, u32[]{:S(2)}, u32[]{:S(2)}) collective-permute-start(f32[24,256]{1,0:T(8,128)S(1)} %add_add_fusion.10), channel_id=1, source_target_pairs={{0,96},{32,64},{64,32},{96,0},{1,97},{33,65},{65,33},{97,1},{2,98}... | collective-permute-start | bytes 73736 | tf_op jit(solution)/shard_map/ppermute | solution.py:566
  59.5 1.1 %collective-permute-start.48 = (f32[24,256]{1,0:T(8,128)S(1)}, f32[24,256]{1,0:T(8,128)S(1)}, u32[]{:S(2)}, u32[]{:S(2)}) collective-permute-start(f32[24,256]{1,0:T(8,128)S(1)} %add_add_fusion.10), channel_id=1, source_target_pairs={{0,64},{32,96},{64,0},{96,32},{1,65},{33,97},{65,1},{97,33},{2,66}... | collective-permute-start | bytes 73736 | tf_op jit(solution)/shard_map/ppermute | solution.py:566
  60.6 0.5 collective-permute-start.49
  61.1 0.9 %collective-permute-done.47 = f32[24,256]{1,0:T(8,128)S(1)} collective-permute-done((f32[24,256]{1,0:T(8,128)S(1)}, f32[24,256]{1,0:T(8,128)S(1)}, u32[]{:S(2)}, u32[]{:S(2)}) %collective-permute-start.47) | collective-permute-done | bytes 24608 | tf_op jit(solution)/shard_map/ppermute | solution.py:566
  62.1 2.7 %collective-permute-done.48 = f32[24,256]{1,0:T(8,128)S(1)} collective-permute-done((f32[24,256]{1,0:T(8,128)S(1)}, f32[24,256]{1,0:T(8,128)S(1)}, u32[]{:S(2)}, u32[]{:S(2)}) %collective-permute-start.48) | collective-permute-done | bytes 24608 | tf_op jit(solution)/shard_map/ppermute | solution.py:566
  64.8 0.0 collective-permute-done.49
  64.8 0.0 copy-start.6
  64.8 0.0 copy-start.7
  64.8 0.0 copy-start.8
  64.8 0.0 copy-start.9
  64.9 3.2 %shard_map.83 = (f32[256,32,128]{2,1,0:T(8,128)}, f32[5,256]{1,0:T(8,128)}, s32[1]{0:T(128)}) custom-call(f32[24,256]{1,0:T(8,128)S(1)} %add_add_fusion.9.sums_ref, f32[2,40,160,128]{3,2,1,0:T(8,128)S(1)} %get-tuple-element.353.v0, f32[2,40,160,128]{3,2,1,0:T(8,128)S(1)} %get-tuple-element.354.v1, f32[2,40,160,128]{3,2,1,0:T(8,128)S(1)} %get-tuple-element.355.v2, ...), custom_call_target="tpu_custom_call" | custom-call | tf_op jit(solution)/shard_map/pallas_call | solution.py:543
  68.6 0.0 copy-done.6
  68.6 0.0 copy-done.7
  68.6 0.0 copy-done.8
  68.6 0.0 copy-done.9
  68.6 0.2 conditional.1
  (4 shorter events, 0.0 us)
Async XLA Ops:
  4.8 7.1 %collective-permute-start.36 = (f32[17,8,256]{2,1,0:T(8,128)S(1)}, f32[17,8,256]{2,1,0:T(8,128)S(1)}, u32[]{:S(2)}, u32[]{:S(2)}) collective-permute-start(f32[17,8,256]{2,1,0:T(8,128)S(1)} %get-tuple-element.334), channel_id=1, source_target_pairs={{0,1},{1,0},{2,3},{3,2},{4,5},{5,4},{6,7},{7,6},{8,9},{9,8},{10,11... | collective-permute-start | bytes 417800 | tf_op jit(solution)/shard_map/ppermute | solution.py:70
  6.9 5.0 %collective-permute-start.37 = (f32[17,8,256]{2,1,0:T(8,128)S(1)}, f32[17,8,256]{2,1,0:T(8,128)S(1)}, u32[]{:S(2)}, u32[]{:S(2)}) collective-permute-start(f32[17,8,256]{2,1,0:T(8,128)S(1)} %get-tuple-element.335), channel_id=1, source_target_pairs={{1,2},{3,4},{5,6},{7,8},{9,10},{11,12},{13,14},{2,1},{4,3},{6,5},{... | collective-permute-start | bytes 417800 | tf_op jit(solution)/shard_map/ppermute | solution.py:71
  12.0 15.2 %collective-permute-start.38 = (f32[77,8,256]{2,1,0:T(8,128)S(1)}, f32[77,8,256]{2,1,0:T(8,128)S(1)}, u32[]{:S(2)}, u32[]{:S(2)}) collective-permute-start(f32[77,8,256]{2,1,0:T(8,128)S(1)} %get-tuple-element.337), channel_id=1, source_target_pairs={{0,16},{16,0},{32,48},{48,32},{64,80},{80,64},{96,112},{112,96},{1... | collective-permute-start | bytes 1892360 | tf_op jit(solution)/shard_map/ppermute | solution.py:70
  12.1 15.1 %collective-permute-start.39 = (f32[77,8,256]{2,1,0:T(8,128)S(1)}, f32[77,8,256]{2,1,0:T(8,128)S(1)}, u32[]{:S(2)}, u32[]{:S(2)}) collective-permute-start(f32[77,8,256]{2,1,0:T(8,128)S(1)} %get-tuple-element.338), channel_id=1, source_target_pairs={{16,32},{48,64},{80,96},{32,16},{64,48},{96,80},{17,33},{49,65},{8... | collective-permute-start | bytes 1892360 | tf_op jit(solution)/shard_map/ppermute | solution.py:71
  33.4 3.7 %collective-permute-start.40 = (f32[24,256]{1,0:T(8,128)S(1)}, f32[24,256]{1,0:T(8,128)S(1)}, u32[]{:S(2)}, u32[]{:S(2)}) collective-permute-start(f32[24,256]{1,0:T(8,128)S(1)} %get-tuple-element.352), channel_id=1, source_target_pairs={{0,16},{16,0},{1,17},{17,1},{2,18},{18,2},{3,19},{19,3},{4,20},{20... | collective-permute-start | bytes 73736 | tf_op jit(solution)/shard_map/ppermute | solution.py:566
  37.2 8.4 %collective-permute-start.41 = (f32[24,256]{1,0:T(8,128)S(1)}, f32[24,256]{1,0:T(8,128)S(1)}, u32[]{:S(2)}, u32[]{:S(2)}) collective-permute-start(f32[24,256]{1,0:T(8,128)S(1)} %add.458), channel_id=1, source_target_pairs={{0,3},{1,2},{2,1},{3,0},{4,7},{5,6},{6,5},{7,4},{8,11},{9,10},{10,... | collective-permute-start | bytes 73736 | tf_op jit(solution)/shard_map/ppermute | solution.py:566
  43.8 5.3 %collective-permute-start.42 = (f32[24,256]{1,0:T(8,128)S(1)}, f32[24,256]{1,0:T(8,128)S(1)}, u32[]{:S(2)}, u32[]{:S(2)}) collective-permute-start(f32[24,256]{1,0:T(8,128)S(1)} %add.458), channel_id=1, source_target_pairs={{0,2},{1,3},{2,0},{3,1},{4,6},{5,7},{6,4},{7,5},{8,10},{9,11},{10,... | collective-permute-start | bytes 73736 | tf_op jit(solution)/shard_map/ppermute | solution.py:566
  44.0 5.1 %collective-permute-start.43 = (f32[24,256]{1,0:T(8,128)S(1)}, f32[24,256]{1,0:T(8,128)S(1)}, u32[]{:S(2)}, u32[]{:S(2)}) collective-permute-start(f32[24,256]{1,0:T(8,128)S(1)} %add.458), channel_id=1, source_target_pairs={{0,1},{1,0},{2,3},{3,2},{4,5},{5,4},{6,7},{7,6},{8,9},{9,8},{10,11... | collective-permute-start | bytes 73736 | tf_op jit(solution)/shard_map/ppermute | solution.py:566
  49.1 5.1 %collective-permute-start.44 = (f32[24,256]{1,0:T(8,128)S(1)}, f32[24,256]{1,0:T(8,128)S(1)}, u32[]{:S(2)}, u32[]{:S(2)}) collective-permute-start(f32[24,256]{1,0:T(8,128)S(1)} %add_add_fusion.11), channel_id=1, source_target_pairs={{0,12},{4,8},{8,4},{12,0},{1,13},{5,9},{9,5},{13,1},{2,14},{6,10},... | collective-permute-start | bytes 73736 | tf_op jit(solution)/shard_map/ppermute | solution.py:566
  51.0 5.3 %collective-permute-start.45 = (f32[24,256]{1,0:T(8,128)S(1)}, f32[24,256]{1,0:T(8,128)S(1)}, u32[]{:S(2)}, u32[]{:S(2)}) collective-permute-start(f32[24,256]{1,0:T(8,128)S(1)} %add_add_fusion.11), channel_id=1, source_target_pairs={{0,8},{4,12},{8,0},{12,4},{1,9},{5,13},{9,1},{13,5},{2,10},{6,14},... | collective-permute-start | bytes 73736 | tf_op jit(solution)/shard_map/ppermute | solution.py:566
  52.8 3.8 %collective-permute-start.46 = (f32[24,256]{1,0:T(8,128)S(1)}, f32[24,256]{1,0:T(8,128)S(1)}, u32[]{:S(2)}, u32[]{:S(2)}) collective-permute-start(f32[24,256]{1,0:T(8,128)S(1)} %add_add_fusion.11), channel_id=1, source_target_pairs={{0,4},{4,0},{8,12},{12,8},{1,5},{5,1},{9,13},{13,9},{2,6},{6,2},{1... | collective-permute-start | bytes 73736 | tf_op jit(solution)/shard_map/ppermute | solution.py:566
  56.7 5.4 %collective-permute-start.47 = (f32[24,256]{1,0:T(8,128)S(1)}, f32[24,256]{1,0:T(8,128)S(1)}, u32[]{:S(2)}, u32[]{:S(2)}) collective-permute-start(f32[24,256]{1,0:T(8,128)S(1)} %add_add_fusion.10), channel_id=1, source_target_pairs={{0,96},{32,64},{64,32},{96,0},{1,97},{33,65},{65,33},{97,1},{2,98}... | collective-permute-start | bytes 73736 | tf_op jit(solution)/shard_map/ppermute | solution.py:566
  59.5 5.3 %collective-permute-start.48 = (f32[24,256]{1,0:T(8,128)S(1)}, f32[24,256]{1,0:T(8,128)S(1)}, u32[]{:S(2)}, u32[]{:S(2)}) collective-permute-start(f32[24,256]{1,0:T(8,128)S(1)} %add_add_fusion.10), channel_id=1, source_target_pairs={{0,64},{32,96},{64,0},{96,32},{1,65},{33,97},{65,1},{97,33},{2,66}... | collective-permute-start | bytes 73736 | tf_op jit(solution)/shard_map/ppermute | solution.py:566
  60.6 4.2 %collective-permute-start.49 = (f32[24,256]{1,0:T(8,128)S(1)}, f32[24,256]{1,0:T(8,128)S(1)}, u32[]{:S(2)}, u32[]{:S(2)}) collective-permute-start(f32[24,256]{1,0:T(8,128)S(1)} %add_add_fusion.10), channel_id=1, source_target_pairs={{0,32},{32,0},{64,96},{96,64},{1,33},{33,1},{65,97},{97,65},{2,34}... | collective-permute-start | bytes 73736 | tf_op jit(solution)/shard_map/ppermute | solution.py:566
  64.8 3.8 %copy-start.6 = (s32[32,128]{1,0:T(8,128)S(1)}, s32[32,128]{1,0:T(8,128)}, u32[]{:S(2)}) copy-start(s32[32,128]{1,0:T(8,128)} %eh_hbm.1) | copy-start | bytes 49156
  64.8 3.8 %copy-start.7 = (s32[32,128]{1,0:T(8,128)S(1)}, s32[32,128]{1,0:T(8,128)}, u32[]{:S(2)}) copy-start(s32[32,128]{1,0:T(8,128)} %ev_hbm.1) | copy-start | bytes 49156
  64.8 3.8 %copy-start.8 = (s32[32,128]{1,0:T(8,128)S(1)}, s32[32,128]{1,0:T(8,128)}, u32[]{:S(2)}) copy-start(s32[32,128]{1,0:T(8,128)} %pads_hbm.1) | copy-start | bytes 49156
  64.8 3.8 %copy-start.9 = (f32[256,8]{0,1:T(8,128)S(1)}, f32[256,8]{0,1:T(8,128)}, u32[]{:S(2)}) copy-start(f32[256,8]{0,1:T(8,128)} %param.16) | copy-start | bytes 24580
